TPU v7x, 32 devices: a whole 2x2x4 slice. The times are simulated.
32 devices in a mesh: groups: 2 (over y), dp: 8 (over z, x), tensor: 2 (over core).
Axes of the slice: x: 2, y: 2, z: 4, core: 2. Of those that a mesh axis runs over, the one named last changes fastest.
Arguments:
- queries: bfloat16 [2048, 8192], P(('groups', 'dp'), 'tensor'), parts along dimension 0, may hold values from -14 to 14
- answer_prompt: int32 [2048, 1], P(('groups', 'dp')), parts along dimension 0, may hold values from 0 to 7; in each aligned block of 128 rows (0 to 127, 128 to 255, ...) at most 32 rows name the same one
- prompt_owner: int32 [16], P('groups'), parts along dimension 0, may hold values from 0 to 7, each once
- context_keys: bfloat16 [16384, 1024], P(('groups', 'dp'), 'tensor'), parts along dimension 0, may hold values from -8 to 8
- context_values: bfloat16 [16384, 1024], P(('groups', 'dp'), 'tensor'), parts along dimension 0, may hold values from -6 to 6
- score_weight: float32 [8192], P('tensor'), may hold values from -6 to 6
Outputs:
- token_score: float32 [2048], P(('groups', 'dp')), parts along dimension 0
There are 2 independent parts, one for each index of `groups`. A program takes and returns all parts, laid end to end along the dimension named above; an argument that names none is the same for every part. Nothing has to cross between parts.
Inputs may be any that keep to these rules, and one draw needn't show every extreme that they name: `answer_prompt`: among the 128 answer tokens of one replica at most 32 name the same prompt, and 32 is reached; every prompt is named by some token. `prompt_owner`: each replica holds exactly one prompt's context.
All inputs are finite; a program needn't handle non-finite values.
Results may differ from a plain program's by a relative error of at most 0.0042.
Values may be sent and summed in bfloat16 or wider, within the bound.
No kernel may reach another device: no remote copies, remote signals or barrier semaphores. Data moves between devices by JAX's collectives and lax.ppermute only.
A program may use at most 64 MiB of HBM per device.

v0:
```python
import math

import jax
import jax.numpy as jnp
from jax import lax
from jax.sharding import PartitionSpec as P

HD = 128


def attend(query_rows, key_rows, value_rows):
    row_count, feature_width = query_rows.shape
    context_len = key_rows.shape[0]
    kv_local = key_rows.shape[1] // HD
    group_size = feature_width // HD // kv_local
    query_heads = query_rows.reshape(row_count, kv_local, group_size, HD).transpose(1, 0, 2, 3)
    query_heads = query_heads.reshape(kv_local, row_count * group_size, HD)
    key_heads = key_rows.reshape(context_len, kv_local, HD).transpose(1, 0, 2)
    value_heads = value_rows.reshape(context_len, kv_local, HD).transpose(1, 0, 2)

    def per_head(packed):
        logits = lax.dot_general(
            packed[0], packed[1], (((1,), (1,)), ((), ())), preferred_element_type=jnp.float32
        )
        logits = logits * (1.0 / math.sqrt(HD))
        row_peak = jnp.max(logits, axis=1, keepdims=True)
        exponent = jnp.exp(logits - row_peak)
        weights = (exponent / jnp.sum(exponent, axis=1, keepdims=True)).astype(jnp.bfloat16)
        return jnp.dot(weights, packed[2], preferred_element_type=jnp.float32).astype(jnp.bfloat16)

    attended = lax.map(per_head, (query_heads, key_heads, value_heads))
    attended = attended.reshape(kv_local, row_count, group_size, HD).transpose(1, 0, 2, 3)
    return attended.reshape(row_count, feature_width)


def on_device(queries, answer_prompt, prompt_owner, context_keys, context_values, score_weight):
    tok_rows, feature_width = queries.shape
    peer_count = lax.axis_size("dp")
    capacity = max(2, 2 * tok_rows // peer_count)
    prompt_hits = answer_prompt == jnp.arange(prompt_owner.shape[0], dtype=jnp.int32)[None, :]
    target = jnp.sum(jnp.where(prompt_hits, prompt_owner[None, :], 0), axis=1)
    dest_hits = (target[:, None] == jnp.arange(peer_count, dtype=jnp.int32)[None, :]).astype(
        jnp.int32
    )
    earlier = jnp.cumsum(dest_hits, axis=0) - dest_hits
    rank_in = jnp.sum(earlier * dest_hits, axis=1)
    slot_index = target * capacity + rank_in
    outgoing = (
        jnp.zeros((peer_count * capacity, feature_width), jnp.bfloat16).at[slot_index].set(queries)
    )
    outgoing = outgoing.reshape(peer_count, capacity, feature_width)
    arrived = lax.all_to_all(outgoing, "dp", split_axis=0, concat_axis=0, tiled=True)
    sources = arrived.shape[0]
    slot_items = arrived.shape[1]
    attended = attend(
        arrived.reshape(sources * slot_items, feature_width), context_keys, context_values
    )
    returned = lax.all_to_all(
        attended.reshape(sources, slot_items, feature_width),
        "dp",
        split_axis=0,
        concat_axis=0,
        tiled=True,
    )
    own_rows = returned.reshape(peer_count * capacity, feature_width)[slot_index]
    head_terms = jnp.sum(own_rows.astype(jnp.float32) * score_weight[None, :], axis=1)
    return lax.psum(head_terms, "tensor")


def solution(mesh):
    return jax.shard_map(
        on_device,
        mesh=mesh,
        in_specs=(
            P(("groups", "dp"), "tensor"),
            P(("groups", "dp"), None),
            P("groups"),
            P(("groups", "dp"), "tensor"),
            P(("groups", "dp"), "tensor"),
            P("tensor"),
        ),
        out_specs=P(("groups", "dp")),
        check_vma=False,
    )
```

profile of v0, /device:TPU:0, one launch (start us, length us, event | category | flops | bytes accessed | tf_op | source)
XLA Modules:
  0.0 149.6 jit_solution(8681602909557494726)
XLA Ops:
  1.3 4.3 %scatter_custom_fusion = bf16[256,4096]{1,0:T(8,128)(2,1)} fusion(s32[128]{0:T(128)S(1)} %fusion.18, bf16[128,4096]{1,0:T(8,128)(2,1)} %param.8, bf16[]{:T(256)} %constant.7.clone.1), kind=kCustom, calls=%fused_computation.22 | custom fusion | bytes 2097664 | tf_op jit(solution)/shard_map/scatter | solution.py:49
  5.6 7.3 %all-to-all-start = ((bf16[8,32,4096]{2,1,0:T(8,128)(2,1)}), bf16[8,32,4096]{2,1,0:T(8,128)(2,1)S(1)}, u32[]{:S(2)}, u32[]{:S(2)}) async-start(bf16[8,32,4096]{2,1,0:T(8,128)(2,1)} %bitcast.57), calls=%async_computation | async-start | bytes 4194304 | tf_op jit(solution)/shard_map/all_to_all | solution.py:52
  12.9 1.5 copy.14
  14.3 2.3 %copy.15 = bf16[1024,512]{0,1:T(8,128)(2,1)} copy(bf16[1024,512]{1,0:T(8,128)(2,1)} %param.12) | data formatting | bytes 2097152 | tf_op args[4]
  16.6 44.5 %all-to-all-done = bf16[8,32,4096]{2,1,0:T(8,128)(2,1)S(1)} async-done(((bf16[8,32,4096]{2,1,0:T(8,128)(2,1)}), bf16[8,32,4096]{2,1,0:T(8,128)(2,1)S(1)}, u32[]{:S(2)}, u32[]{:S(2)}) %all-to-all-start) | async-done | bytes 2097184 | tf_op jit(solution)/shard_map/all_to_all | solution.py:52
  62.0 26.9 %while.10 = (s32[]{:T(128)}, bf16[4,2048,128]{2,1,0:T(8,128)(2,1)}, bf16[4,2048,128]{2,1,0:T(8,128)(2,1)S(1)}, bf16[4,1024,128]{1,2,0:T(8,128)(2,1)S(1)}, bf16[4,1024,128]{1,2,0:T(8,128)(2,1)}, /*index=5*/s32[]{:T(128)}) while((s32[]{:T(128)}, bf16[4,2048,128]{2,1,0:T(8,128)(2,1)}, bf16[4,2048,128]{2,1,0:T(8,128)(2,1)S(1)}, ...), condition=%wide.region_7.8_spmd, body=%wide.region_4.7_spmd.sunk | while | flops 1092874240 | bytes 26781764 | solution.py:31
  62.0 1.3 multiply_reduce_fusion.3
  63.3 1.4 fusion.23
  64.7 4.0 %fusion.24 = bf16[4,2048,128]{2,1,0:T(8,128)(2,1)} fusion(bf16[4,2048,128]{2,1,0:T(8,128)(2,1)} %get-tuple-element.97, s32[]{:T(128)} %get-tuple-element.96, f32[2048,1024]{0,1:T(8,128)S(1)} %get-tuple-element.88, f32[2048]{0:T(1024)S(1)} %fusion.23, f32[2048]{0:T(1024)S(1)} %get-tuple-element.89, bf16[4,1024,128]{1,2,0:T(8,128)(2,1)} %get-tuple-element.106), kind=kOutput, calls=%fused_computation.9.clone.1 | convolution fusion | flops 545521664 | bytes 9192448 | tf_op jit(solution)/shard_map/while/body/eval_jaxpr/dot_general | solution.py:29
  68.7 1.3 multiply_reduce_fusion.3
  70.0 1.4 fusion.23
  71.4 4.0 %fusion.24 = bf16[4,2048,128]{2,1,0:T(8,128)(2,1)} fusion(bf16[4,2048,128]{2,1,0:T(8,128)(2,1)} %get-tuple-element.97, s32[]{:T(128)} %get-tuple-element.96, f32[2048,1024]{0,1:T(8,128)S(1)} %get-tuple-element.88, f32[2048]{0:T(1024)S(1)} %fusion.23, f32[2048]{0:T(1024)S(1)} %get-tuple-element.89, bf16[4,1024,128]{1,2,0:T(8,128)(2,1)} %get-tuple-element.106), kind=kOutput, calls=%fused_computation.9.clone.1 | convolution fusion | flops 545521664 | bytes 9192448 | tf_op jit(solution)/shard_map/while/body/eval_jaxpr/dot_general | solution.py:29
  75.4 1.3 multiply_reduce_fusion.3
  76.7 1.4 fusion.23
  78.1 4.0 %fusion.24 = bf16[4,2048,128]{2,1,0:T(8,128)(2,1)} fusion(bf16[4,2048,128]{2,1,0:T(8,128)(2,1)} %get-tuple-element.97, s32[]{:T(128)} %get-tuple-element.96, f32[2048,1024]{0,1:T(8,128)S(1)} %get-tuple-element.88, f32[2048]{0:T(1024)S(1)} %fusion.23, f32[2048]{0:T(1024)S(1)} %get-tuple-element.89, bf16[4,1024,128]{1,2,0:T(8,128)(2,1)} %get-tuple-element.106), kind=kOutput, calls=%fused_computation.9.clone.1 | convolution fusion | flops 545521664 | bytes 9192448 | tf_op jit(solution)/shard_map/while/body/eval_jaxpr/dot_general | solution.py:29
  82.1 1.3 multiply_reduce_fusion.3
  83.4 1.4 fusion.23
  84.8 4.0 %fusion.24 = bf16[4,2048,128]{2,1,0:T(8,128)(2,1)} fusion(bf16[4,2048,128]{2,1,0:T(8,128)(2,1)} %get-tuple-element.97, s32[]{:T(128)} %get-tuple-element.96, f32[2048,1024]{0,1:T(8,128)S(1)} %get-tuple-element.88, f32[2048]{0:T(1024)S(1)} %fusion.23, f32[2048]{0:T(1024)S(1)} %get-tuple-element.89, bf16[4,1024,128]{1,2,0:T(8,128)(2,1)} %get-tuple-element.106), kind=kOutput, calls=%fused_computation.9.clone.1 | convolution fusion | flops 545521664 | bytes 9192448 | tf_op jit(solution)/shard_map/while/body/eval_jaxpr/dot_general | solution.py:29
  88.8 2.0 %copy.18 = bf16[256,4,8,128]{3,2,1,0:T(8,128)(2,1)S(1)} copy(bf16[256,4,8,128]{3,2,0,1:T(8,128)(2,1)} %bitcast.15) | data formatting | bytes 4194304 | tf_op jit(solution)/shard_map/transpose | solution.py:32
  90.8 2.3 %reshape_reshape.7 = bf16[8,32,4096]{2,1,0:T(8,128)(2,1)} reshape(bf16[256,4,8,128]{3,2,1,0:T(8,128)(2,1)S(1)} %copy.18) | data formatting | bytes 4194304 | tf_op jit(solution)/shard_map/reshape;reshape | solution.py:59
  93.1 3.6 %all-to-all-start.1 = ((bf16[8,32,4096]{2,1,0:T(8,128)(2,1)}), bf16[8,32,4096]{2,1,0:T(8,128)(2,1)S(1)}, u32[]{:S(2)}, u32[]{:S(2)}) async-start(bf16[8,32,4096]{2,1,0:T(8,128)(2,1)} %reshape_reshape.7), calls=%async_computation.1 | async-start | bytes 4194304 | tf_op jit(solution)/shard_map/all_to_all | solution.py:58
  96.7 48.4 %all-to-all-done.1 = bf16[8,32,4096]{2,1,0:T(8,128)(2,1)S(1)} async-done(((bf16[8,32,4096]{2,1,0:T(8,128)(2,1)}), bf16[8,32,4096]{2,1,0:T(8,128)(2,1)S(1)}, u32[]{:S(2)}, u32[]{:S(2)}) %all-to-all-start.1) | async-done | bytes 2097184 | tf_op jit(solution)/shard_map/all_to_all | solution.py:58
  145.2 1.2 gather_fusion
  146.7 3.0 %psum.7 = f32[128]{0:T(128)} all-reduce(f32[128]{0:T(128)S(1)} %multiply_reduce_fusion.1), channel_id=1, replica_groups=mesh['groups'=2,'dp'=8,'tensor'=2] {'tensor'}, use_global_device_ids=true, to_apply=%region_9.10 | all-reduce | flops 128 | bytes 1024 | tf_op jit(solution)/shard_map/psum | solution.py:67
  (12 shorter events, 2.4 us)
Async XLA Ops:
  5.6 55.5 %all-to-all-start = ((bf16[8,32,4096]{2,1,0:T(8,128)(2,1)}), bf16[8,32,4096]{2,1,0:T(8,128)(2,1)S(1)}, u32[]{:S(2)}, u32[]{:S(2)}) async-start(bf16[8,32,4096]{2,1,0:T(8,128)(2,1)} %bitcast.57), calls=%async_computation | async-start | bytes 4194304 | tf_op jit(solution)/shard_map/all_to_all | solution.py:52
  93.1 52.0 %all-to-all-start.1 = ((bf16[8,32,4096]{2,1,0:T(8,128)(2,1)}), bf16[8,32,4096]{2,1,0:T(8,128)(2,1)S(1)}, u32[]{:S(2)}, u32[]{:S(2)}) async-start(bf16[8,32,4096]{2,1,0:T(8,128)(2,1)} %reshape_reshape.7), calls=%async_computation.1 | async-start | bytes 4194304 | tf_op jit(solution)/shard_map/all_to_all | solution.py:58
  145.1 1.2 copy-start
where the time goes:
time: 150 us
  waiting for transfers between devices  92.9 us (62%)
  matrix products  21.2 us (14%)
  local copies, waits for them, and re-layouts  14.4 us (10%)
  starting transfers between devices  10.9 us (7%)
  other arithmetic  7.21 us (5%)
  blocking collectives  2.97 us (2%)
    all_to_all x1, waiting for transfers between devices, on_device(): lax.all_to_all(attended.reshape(sources, slot_items, feature_width), 'dp'...  48.4 us
    all_to_all x1, waiting for transfers between devices, on_device(): lax.all_to_all(outgoing, 'dp', split_axis=0, concat_axis=0, tiled=True)  44.5 us
    dot_general x4, matrix products, per_head(): jnp.dot(weights, packed[2], preferred_element_type=jnp.float32)  16 us
    all_to_all x1, starting transfers between devices, on_device(): lax.all_to_all(outgoing, 'dp', split_axis=0, concat_axis=0, tiled=True)  7.25 us
    reduce_sum x4, other arithmetic, per_head(): jnp.sum(exponent, axis=1, keepdims=True)  5.62 us
    dot_general x4, matrix products, per_head(): lax.dot_general(packed[0], packed[1], (((1,), (1,)), ((), ())), preferred...  5.21 us
    scatter x1, local copies, waits for them, and re-layouts, on_device(): jnp.zeros((peer_count * capacity, feature_width), jnp.bfloat16)  4.29 us
    unnamed x5, local copies, waits for them, and re-layouts  4.26 us
  transfers between devices with their start and end apart: 2, of which 2 were waited for; matrix products, arithmetic and copies ran while one was open for 3% of the time, Pallas kernels for 0%

commit v1 on v0

v1 whole, which is shorter than its diff:
```python
import functools
import math

import jax
import jax.numpy as jnp
from jax import lax
from jax.experimental import pallas as pl
from jax.experimental.pallas import tpu as pltpu
from jax.sharding import PartitionSpec as P

HD = 128
SCALE = math.log2(math.e) / math.sqrt(HD)
MAX_PAIRWISE = 16


def route_kernel(capacity, by_xor, me_ref, prompt_ref, owner_ref, query_ref, column_ref, *out_refs):
    tok_rows = prompt_ref.shape[0]
    peers = len(out_refs) if by_xor else out_refs[0].shape[0] // capacity
    prompt_lane = lax.broadcasted_iota(jnp.int32, (tok_rows, owner_ref.shape[1]), 1)
    target = jnp.sum(
        jnp.where(prompt_ref[...] == prompt_lane, owner_ref[...], 0), axis=1, keepdims=True
    )
    peer_lane = lax.broadcasted_iota(jnp.int32, (tok_rows, peers), 1)
    hits = (target == peer_lane).astype(jnp.float32)
    earlier_mask = lax.broadcasted_iota(jnp.int32, (tok_rows, tok_rows), 0) > (
        lax.broadcasted_iota(jnp.int32, (tok_rows, tok_rows), 1)
    )
    earlier = jnp.dot(
        earlier_mask.astype(jnp.bfloat16),
        hits.astype(jnp.bfloat16),
        preferred_element_type=jnp.float32,
    )
    rank = jnp.sum(earlier * hits, axis=1, keepdims=True).astype(jnp.int32)
    place = target ^ me_ref[0] if by_xor else target
    column = place * capacity + rank
    column_ref[...] = column
    slots = peers * capacity
    picks = (column == lax.broadcasted_iota(jnp.int32, (tok_rows, slots), 1)).astype(jnp.float32)
    picks = picks.T.astype(jnp.bfloat16)
    for n, out_ref in enumerate(out_refs):
        rows = out_ref.shape[0]
        out_ref[...] = jnp.dot(
            picks[n * rows : (n + 1) * rows], query_ref[...], preferred_element_type=jnp.float32
        ).astype(jnp.bfloat16)


def route(queries, answer_prompt, prompt_owner, me, peers, capacity, by_xor):
    tok_rows, width = queries.shape
    pieces = peers if by_xor else 1
    piece_rows = peers * capacity // pieces
    step = min(width, 1024)
    return pl.pallas_call(
        functools.partial(route_kernel, capacity, by_xor),
        grid=(width // step,),
        in_specs=[
            pl.BlockSpec(memory_space=pltpu.SMEM),
            pl.BlockSpec((tok_rows, 1), lambda c: (0, 0)),
            pl.BlockSpec((1, prompt_owner.shape[0]), lambda c: (0, 0)),
            pl.BlockSpec((tok_rows, step), lambda c: (0, c)),
        ],
        out_specs=[pl.BlockSpec((tok_rows, 1), lambda c: (0, 0))]
        + [pl.BlockSpec((piece_rows, step), lambda c: (0, c))] * pieces,
        out_shape=[jax.ShapeDtypeStruct((tok_rows, 1), jnp.int32)]
        + [jax.ShapeDtypeStruct((piece_rows, width), jnp.bfloat16)] * pieces,
        name="route",
    )(me.reshape(1), answer_prompt, prompt_owner.reshape(1, -1), queries)


def attend_kernel(group_size, query_ref, key_ref, value_ref, weight_ref, score_ref, total_ref):
    kv_head = pl.program_id(1)
    rows = query_ref.shape[0]
    stacked = jnp.concatenate(
        [query_ref[:, h * HD : (h + 1) * HD] for h in range(group_size)], axis=0
    )
    logits = lax.dot_general(
        stacked, key_ref[...], (((1,), (1,)), ((), ())), preferred_element_type=jnp.float32
    )
    peak = jnp.max(logits, axis=1, keepdims=True)
    exponent = jnp.exp2((logits - peak) * SCALE)
    inverse = 1.0 / jnp.sum(exponent, axis=1, keepdims=True)
    probs = (exponent * inverse).astype(jnp.bfloat16)
    attended = jnp.dot(probs, value_ref[...], preferred_element_type=jnp.float32)
    attended = attended.astype(jnp.bfloat16).astype(jnp.float32)
    total = jnp.zeros((rows, HD), jnp.float32)
    for h in range(group_size):
        total += attended[h * rows : (h + 1) * rows] * weight_ref[:, h * HD : (h + 1) * HD]

    @pl.when(kv_head == 0)
    def _():
        total_ref[...] = total

    @pl.when(kv_head > 0)
    def _():
        total_ref[...] += total

    @pl.when(kv_head == pl.num_programs(1) - 1)
    def _():
        score_ref[0] = jnp.sum(total_ref[...].T, axis=0, keepdims=True)


def attend_score(query_rows, key_rows, value_rows, score_weight):
    row_count, width = query_rows.shape
    context_len, kv_width = key_rows.shape
    kv_local = kv_width // HD
    group_size = width // kv_width
    block = math.gcd(row_count, 32)
    blocks = row_count // block
    flops = 4 * row_count * width * context_len
    return pl.pallas_call(
        functools.partial(attend_kernel, group_size),
        grid=(blocks, kv_local),
        in_specs=[
            pl.BlockSpec((block, group_size * HD), lambda r, g: (r, g)),
            pl.BlockSpec((context_len, HD), lambda r, g: (0, g)),
            pl.BlockSpec((context_len, HD), lambda r, g: (0, g)),
            pl.BlockSpec((1, group_size * HD), lambda r, g: (0, g)),
        ],
        out_specs=pl.BlockSpec((1, 1, block), lambda r, g: (r, 0, 0)),
        out_shape=jax.ShapeDtypeStruct((blocks, 1, block), jnp.float32),
        scratch_shapes=[pltpu.VMEM((block, HD), jnp.float32)],
        cost_estimate=pl.CostEstimate(
            flops=flops,
            bytes_accessed=2 * (row_count * width + 2 * context_len * kv_width),
            transcendentals=row_count * width // HD * context_len,
        ),
        name="attend_score",
    )(query_rows, key_rows, value_rows, score_weight.reshape(1, -1)).reshape(1, row_count)


def on_device(queries, answer_prompt, prompt_owner, context_keys, context_values, score_weight):
    tok_rows, width = queries.shape
    peers = lax.axis_size("dp")
    cores = lax.axis_size("tensor")
    capacity = max(2, 2 * tok_rows // peers)
    by_xor = peers <= MAX_PAIRWISE and peers & (peers - 1) == 0 and capacity % 16 == 0
    column, *pieces = route(
        queries, answer_prompt, prompt_owner, lax.axis_index("dp"), peers, capacity, by_xor
    )
    score = functools.partial(
        attend_score,
        key_rows=context_keys,
        value_rows=context_values,
        score_weight=score_weight,
    )
    if by_xor:
        order = sorted(range(1, peers), reverse=True)
        arrived = {
            s: lax.ppermute(pieces[s], "dp", [(k, k ^ s) for k in range(peers)]) for s in order
        }
        arrived[0] = pieces[0]
        terms = []
        for s in range(peers):
            own = score(arrived[s])
            both = []
            for c in range(cores):
                if s == 0 and c == 0:
                    both.append(own)
                    continue
                both.append(
                    lax.ppermute(
                        own,
                        ("dp", "tensor"),
                        [
                            (k * cores + j, (k ^ s) * cores + (j ^ c))
                            for k in range(peers)
                            for j in range(cores)
                        ],
                    )
                )
            terms.append(sum(both[1:], both[0]))
        returned = jnp.concatenate(terms, axis=1)
        slots = lax.broadcasted_iota(jnp.int32, (tok_rows, peers * capacity), 1)
        return jnp.sum(jnp.where(column == slots, returned, 0.0), axis=1)
    arrived = lax.all_to_all(
        pieces[0].reshape(peers, capacity, width), "dp", split_axis=0, concat_axis=0, tiled=True
    )
    own = score(arrived.reshape(peers * capacity, width))
    returned = lax.all_to_all(
        own.reshape(peers, capacity), "dp", split_axis=0, concat_axis=0, tiled=True
    )
    slots = lax.broadcasted_iota(jnp.int32, (tok_rows, peers * capacity), 1)
    head_terms = jnp.sum(
        jnp.where(column == slots, returned.reshape(1, peers * capacity), 0.0), axis=1
    )
    return lax.psum(head_terms, "tensor")


def solution(mesh):
    return jax.shard_map(
        on_device,
        mesh=mesh,
        in_specs=(
            P(("groups", "dp"), "tensor"),
            P(("groups", "dp"), None),
            P("groups"),
            P(("groups", "dp"), "tensor"),
            P(("groups", "dp"), "tensor"),
            P("tensor"),
        ),
        out_specs=P(("groups", "dp")),
        check_vma=False,
    )
```

time: 150 us -> 99.7 us (0.66)
  waiting for transfers between devices: 92.9 us -> 12.3 us
  Pallas kernels: 0 us -> 47.1 us
  starting transfers between devices: 10.9 us -> 34.4 us
  matrix products: 21.2 us -> 0 us
  local copies, waits for them, and re-layouts: 14.4 us -> 4.16 us
  other arithmetic: 7.21 us -> 0.83 us
  blocking collectives: 2.97 us -> 0 us
    all_to_all x2 -> x0, waiting for transfers between devices: 92.9 us -> none  [the longest x1 48.4 us: on_device(): lax.all_to_all(attended.reshape(sources, slot_items, feature_width), 'dp'...]
    pallas_call x0 -> x9, Pallas kernels: none -> 47.1 us  [the longest x8 41.8 us: attend_score(): pl.pallas_call(functools.partial(attend_kernel, group_size), grid=(blocks...]
    ppermute x0 -> x22, starting transfers between devices: none -> 34.4 us  [the longest x15 21.5 us: on_device(): lax.ppermute(own, ('dp', 'tensor'), [(k * cores + j, (k ^ s) * cores + (j...]
    dot_general x8 -> x0, matrix products: 21.2 us -> none  [the longest x4 16 us: per_head(): jnp.dot(weights, packed[2], preferred_element_type=jnp.float32)]
    ppermute x0 -> x22, waiting for transfers between devices: none -> 12.3 us  [the longest x7 8.01 us: on_device(): lax.ppermute(pieces[s], 'dp', [(k, k ^ s) for k in range(peers)])]
    all_to_all x2 -> x0, starting transfers between devices: 10.9 us -> none  [the longest x1 7.25 us: on_device(): lax.all_to_all(outgoing, 'dp', split_axis=0, concat_axis=0, tiled=True)]
    reduce_sum x7 -> x1, other arithmetic: 6.93 us -> 0.7 us  [on_device(): return jnp.sum(jnp.where(column == slots, returned, 0.0), axis=1)]
    scatter x1 -> x0, local copies, waits for them, and re-layouts: 4.29 us -> none  [on_device(): jnp.zeros((peer_count * capacity, feature_width), jnp.bfloat16)]
  transfers between devices with their start and end apart: 2 -> 22, of which waited for: 2 -> 3; matrix products, arithmetic and copies ran while one was open for 3% -> 0% of each run, Pallas kernels for 0% -> 42%
where the time goes in v1:
time: 99.7 us; the launch traced here: 99 us
  Pallas kernels  47.1 us (47%)
  starting transfers between devices  34.4 us (35%)
  waiting for transfers between devices  12.3 us (12%)
  local copies, waits for them, and re-layouts  4.16 us (4%)
    pallas_call x8, Pallas kernels, attend_score(): pl.pallas_call(functools.partial(attend_kernel, group_size), grid=(blocks...  41.8 us
    ppermute x15, starting transfers between devices, on_device(): lax.ppermute(own, ('dp', 'tensor'), [(k * cores + j, (k ^ s) * cores + (j...  21.5 us
    ppermute x7, starting transfers between devices, on_device(): lax.ppermute(pieces[s], 'dp', [(k, k ^ s) for k in range(peers)])  13 us
    ppermute x7, waiting for transfers between devices, on_device(): lax.ppermute(pieces[s], 'dp', [(k, k ^ s) for k in range(peers)])  8.01 us
    pallas_call x1, Pallas kernels, route(): pl.pallas_call(functools.partial(route_kernel, capacity, by_xor), grid=(w...  5.33 us
    ppermute x15, waiting for transfers between devices, on_device(): lax.ppermute(own, ('dp', 'tensor'), [(k * cores + j, (k ^ s) * cores + (j...  4.27 us
    unnamed x45, local copies, waits for them, and re-layouts  4.06 us
  transfers between devices with their start and end apart: 22, of which 3 were waited for; matrix products, arithmetic and copies ran while one was open for 0% of the time, Pallas kernels for 42%

profile of v1, /device:TPU:0, one launch (start us, length us, event | category | flops | bytes accessed | tf_op | source)
XLA Modules:
  0.0 99.0 jit_solution(3939119295440975939)
XLA Ops:
  1.4 5.3 %route.1 = (s32[128,1]{1,0:T(8,128)}, bf16[32,4096]{1,0:T(8,128)(2,1)}, bf16[32,4096]{1,0:T(8,128)(2,1)}, bf16[32,4096]{1,0:T(8,128)(2,1)}, bf16[32,4096]{1,0:T(...) custom-call(s32[1]{0:T(128)} %bitcast.me_ref, ...), custom_call_target="tpu_custom_call" | custom-call | tf_op jit(solution)/shard_map/route/pallas_call | solution.py:52
  6.7 3.0 %collective-permute-start.1 = (bf16[32,4096]{1,0:T(8,128)(2,1)}, bf16[32,4096]{1,0:T(8,128)(2,1)S(1)}, u32[]{:S(2)}, u32[]{:S(2)}) collective-permute-start(bf16[32,4096]{1,0:T(8,128)(2,1)} %get-tuple-element.16), channel_id=1, source_target_pairs={{0,2},{2,0},{4,6},{6,4},{8,10},{10,8},{12,14},{14,12},{1,3},{3,1},... | collective-permute-start | bytes 786440 | tf_op jit(solution)/shard_map/ppermute | solution.py:148
  9.7 1.6 %collective-permute-start.4 = (bf16[32,4096]{1,0:T(8,128)(2,1)}, bf16[32,4096]{1,0:T(8,128)(2,1)S(1)}, u32[]{:S(2)}, u32[]{:S(2)}) collective-permute-start(bf16[32,4096]{1,0:T(8,128)(2,1)} %get-tuple-element.17), channel_id=1, source_target_pairs={{0,4},{2,6},{4,0},{6,2},{8,12},{10,14},{12,8},{14,10},{1,5},{3,7},... | collective-permute-start | bytes 786440 | tf_op jit(solution)/shard_map/ppermute | solution.py:148
  11.3 5.3 %attend_score.8 = f32[1,1,32]{2,1,0:T(1,128)} custom-call(bf16[32,4096]{1,0:T(8,128)(2,1)} %get-tuple-element.15.query_ref, bf16[1024,512]{1,0:T(8,128)(2,1)} %key_ref.15, bf16[1024,512]{1,0:T(8,128)(2,1)} %value_ref.15, f32[1,4096]{1,0:T(1,128)} %bitcast.13), custom_call_target="tpu_custom_call" | custom-call | flops 536870912 | bytes 2359296 | tf_op jit(solution)/shard_map/attend_score/pallas_call | solution.py:109
  17.3 3.0 %collective-permute-start.10 = (bf16[32,4096]{1,0:T(8,128)(2,1)S(1)}, bf16[32,4096]{1,0:T(8,128)(2,1)S(1)}, u32[]{:S(2)}, u32[]{:S(2)}) collective-permute-start(bf16[32,4096]{1,0:T(8,128)(2,1)S(1)} %copy-done.20), channel_id=1, source_target_pairs={{0,8},{2,10},{4,12},{6,14},{8,0},{10,2},{12,4},{14,6},{1,9},{3,11}... | collective-permute-start | bytes 786440 | tf_op jit(solution)/shard_map/ppermute | solution.py:148
  21.8 3.7 %collective-permute-start.16 = (bf16[32,4096]{1,0:T(8,128)(2,1)S(1)}, bf16[32,4096]{1,0:T(8,128)(2,1)S(1)}, u32[]{:S(2)}, u32[]{:S(2)}) collective-permute-start(bf16[32,4096]{1,0:T(8,128)(2,1)S(1)} %copy-done.18), channel_id=1, source_target_pairs={{0,12},{2,14},{4,8},{6,10},{8,4},{10,6},{12,0},{14,2},{1,13},{3,15... | collective-permute-start | bytes 786440 | tf_op jit(solution)/shard_map/ppermute | solution.py:148
  25.9 5.2 %attend_score.9 = f32[1,1,32]{2,1,0:T(1,128)} custom-call(bf16[32,4096]{1,0:T(8,128)(2,1)} %copy-done.4, bf16[1024,512]{1,0:T(8,128)(2,1)} %key_ref.15, bf16[1024,512]{1,0:T(8,128)(2,1)} %value_ref.15, f32[1,4096]{1,0:T(1,128)} %bitcast.14), custom_call_target="tpu_custom_call" | custom-call | flops 536870912 | bytes 2359296 | tf_op jit(solution)/shard_map/attend_score/pallas_call | solution.py:109
  31.0 5.2 %attend_score.10 = f32[1,1,32]{2,1,0:T(1,128)} custom-call(bf16[32,4096]{1,0:T(8,128)(2,1)} %copy-done.5, bf16[1024,512]{1,0:T(8,128)(2,1)} %key_ref.15, bf16[1024,512]{1,0:T(8,128)(2,1)} %value_ref.15, f32[1,4096]{1,0:T(1,128)} %bitcast.15), custom_call_target="tpu_custom_call" | custom-call | flops 536870912 | bytes 2359296 | tf_op jit(solution)/shard_map/attend_score/pallas_call | solution.py:109
  37.1 5.2 %attend_score.11 = f32[1,1,32]{2,1,0:T(1,128)} custom-call(bf16[32,4096]{1,0:T(8,128)(2,1)} %copy-done.6, bf16[1024,512]{1,0:T(8,128)(2,1)} %key_ref.15, bf16[1024,512]{1,0:T(8,128)(2,1)} %value_ref.15, f32[1,4096]{1,0:T(1,128)} %bitcast.16), custom_call_target="tpu_custom_call" | custom-call | flops 536870912 | bytes 2359296 | tf_op jit(solution)/shard_map/attend_score/pallas_call | solution.py:109
  42.3 1.3 %collective-permute-start.2 = (f32[1,32]{1,0:T(1,128)S(1)}, f32[1,32]{1,0:T(1,128)S(1)}, u32[]{:S(2)}, u32[]{:S(2)}) collective-permute-start(f32[1,32]{1,0:T(1,128)S(1)} %bitcast.36), channel_id=1, source_target_pairs={{0,2},{1,3},{2,0},{3,1},{4,6},{5,7},{6,4},{7,5},{8,10},{9,11},{10,... | collective-permute-start | bytes 392 | tf_op jit(solution)/shard_map/ppermute | solution.py:160
  43.6 5.2 %attend_score.12 = f32[1,1,32]{2,1,0:T(1,128)} custom-call(bf16[32,4096]{1,0:T(8,128)(2,1)} %copy-done.1, bf16[1024,512]{1,0:T(8,128)(2,1)} %key_ref.15, bf16[1024,512]{1,0:T(8,128)(2,1)} %value_ref.15, f32[1,4096]{1,0:T(1,128)} %bitcast.17), custom_call_target="tpu_custom_call" | custom-call | flops 536870912 | bytes 2359296 | tf_op jit(solution)/shard_map/attend_score/pallas_call | solution.py:109
  48.8 8.0 %collective-permute-done.13.query_ref = bf16[32,4096]{1,0:T(8,128)(2,1)S(1)} collective-permute-done((bf16[32,4096]{1,0:T(8,128)(2,1)S(1)}, bf16[32,4096]{1,0:T(8,128)(2,1)S(1)}, u32[]{:S(2)}, u32[]{:S(2)}) %collective-permute-start.13) | collective-permute-done | bytes 262176 | tf_op jit(solution)/shard_map/ppermute | solution.py:148
  57.5 5.2 %attend_score.13 = f32[1,1,32]{2,1,0:T(1,128)} custom-call(bf16[32,4096]{1,0:T(8,128)(2,1)} %copy-done.2, bf16[1024,512]{1,0:T(8,128)(2,1)} %key_ref.15, bf16[1024,512]{1,0:T(8,128)(2,1)} %value_ref.15, f32[1,4096]{1,0:T(1,128)} %bitcast.18), custom_call_target="tpu_custom_call" | custom-call | flops 536870912 | bytes 2359296 | tf_op jit(solution)/shard_map/attend_score/pallas_call | solution.py:109
  63.8 5.2 %attend_score.14 = f32[1,1,32]{2,1,0:T(1,128)} custom-call(bf16[32,4096]{1,0:T(8,128)(2,1)} %copy-done, bf16[1024,512]{1,0:T(8,128)(2,1)} %key_ref.15, bf16[1024,512]{1,0:T(8,128)(2,1)} %value_ref.15, f32[1,4096]{1,0:T(1,128)} %bitcast.19), custom_call_target="tpu_custom_call" | custom-call | flops 536870912 | bytes 2359296 | tf_op jit(solution)/shard_map/attend_score/pallas_call | solution.py:109
  69.7 1.5 %collective-permute-start.9 = (f32[1,32]{1,0:T(1,128)S(1)}, f32[1,32]{1,0:T(1,128)S(1)}, u32[]{:S(2)}, u32[]{:S(2)}) collective-permute-start(f32[1,32]{1,0:T(1,128)S(1)} %bitcast.31), channel_id=1, source_target_pairs={{0,7},{1,6},{2,5},{3,4},{4,3},{5,2},{6,1},{7,0},{8,15},{9,14},{10,... | collective-permute-start | bytes 392 | tf_op jit(solution)/shard_map/ppermute | solution.py:160
  71.2 5.2 %attend_score.15 = f32[1,1,32]{2,1,0:T(1,128)} custom-call(bf16[32,4096]{1,0:T(8,128)(2,1)} %copy-done.3, bf16[1024,512]{1,0:T(8,128)(2,1)} %key_ref.15, bf16[1024,512]{1,0:T(8,128)(2,1)} %value_ref.15, f32[1,4096]{1,0:T(1,128)} %bitcast.20), custom_call_target="tpu_custom_call" | custom-call | flops 536870912 | bytes 2359296 | tf_op jit(solution)/shard_map/attend_score/pallas_call | solution.py:109
  76.4 1.8 %collective-permute-start.8 = (f32[1,32]{1,0:T(1,128)S(1)}, f32[1,32]{1,0:T(1,128)S(1)}, u32[]{:S(2)}, u32[]{:S(2)}) collective-permute-start(f32[1,32]{1,0:T(1,128)S(1)} %bitcast.32), channel_id=1, source_target_pairs={{0,6},{1,7},{2,4},{3,5},{4,2},{5,3},{6,0},{7,1},{8,14},{9,15},{10,... | collective-permute-start | bytes 392 | tf_op jit(solution)/shard_map/ppermute | solution.py:160
  78.1 2.5 %collective-permute-start.12 = (f32[1,32]{1,0:T(1,128)S(1)}, f32[1,32]{1,0:T(1,128)S(1)}, u32[]{:S(2)}, u32[]{:S(2)}) collective-permute-start(f32[1,32]{1,0:T(1,128)S(1)} %bitcast.29), channel_id=1, source_target_pairs={{0,9},{1,8},{2,11},{3,10},{4,13},{5,12},{6,15},{7,14},{8,1},{9,0},... | collective-permute-start | bytes 392 | tf_op jit(solution)/shard_map/ppermute | solution.py:160
  81.6 2.5 %collective-permute-start.15 = (f32[1,32]{1,0:T(1,128)S(1)}, f32[1,32]{1,0:T(1,128)S(1)}, u32[]{:S(2)}, u32[]{:S(2)}) collective-permute-start(f32[1,32]{1,0:T(1,128)S(1)} %bitcast.23), channel_id=1, source_target_pairs={{0,11},{1,10},{2,9},{3,8},{4,15},{5,14},{6,13},{7,12},{8,3},{9,2},... | collective-permute-start | bytes 392 | tf_op jit(solution)/shard_map/ppermute | solution.py:160
  84.1 1.7 %collective-permute-start.14 = (f32[1,32]{1,0:T(1,128)S(1)}, f32[1,32]{1,0:T(1,128)S(1)}, u32[]{:S(2)}, u32[]{:S(2)}) collective-permute-start(f32[1,32]{1,0:T(1,128)S(1)} %bitcast.24), channel_id=1, source_target_pairs={{0,10},{1,11},{2,8},{3,9},{4,14},{5,15},{6,12},{7,13},{8,2},{9,3},... | collective-permute-start | bytes 392 | tf_op jit(solution)/shard_map/ppermute | solution.py:160
  87.1 1.8 %collective-permute-start.17 = (f32[1,32]{1,0:T(1,128)S(1)}, f32[1,32]{1,0:T(1,128)S(1)}, u32[]{:S(2)}, u32[]{:S(2)}) collective-permute-start(f32[1,32]{1,0:T(1,128)S(1)} %bitcast.26), channel_id=1, source_target_pairs={{0,12},{1,13},{2,14},{3,15},{4,8},{5,9},{6,10},{7,11},{8,4},{9,5},... | collective-permute-start | bytes 392 | tf_op jit(solution)/shard_map/ppermute | solution.py:160
  88.9 3.0 %collective-permute-start.21 = (f32[1,32]{1,0:T(1,128)S(1)}, f32[1,32]{1,0:T(1,128)S(1)}, u32[]{:S(2)}, u32[]{:S(2)}) collective-permute-start(f32[1,32]{1,0:T(1,128)S(1)} %bitcast.27), channel_id=1, source_target_pairs={{0,15},{1,14},{2,13},{3,12},{4,11},{5,10},{6,9},{7,8},{8,7},{9,6},... | collective-permute-start | bytes 392 | tf_op jit(solution)/shard_map/ppermute | solution.py:160
  91.9 2.0 %collective-permute-start.20 = (f32[1,32]{1,0:T(1,128)S(1)}, f32[1,32]{1,0:T(1,128)S(1)}, u32[]{:S(2)}, u32[]{:S(2)}) collective-permute-start(f32[1,32]{1,0:T(1,128)S(1)} %bitcast.28), channel_id=1, source_target_pairs={{0,14},{1,15},{2,12},{3,13},{4,10},{5,11},{6,8},{7,9},{8,6},{9,7},... | collective-permute-start | bytes 392 | tf_op jit(solution)/shard_map/ppermute | solution.py:160
  94.5 3.6 %collective-permute-done.20 = f32[1,32]{1,0:T(1,128)S(1)} collective-permute-done((f32[1,32]{1,0:T(1,128)S(1)}, f32[1,32]{1,0:T(1,128)S(1)}, u32[]{:S(2)}, u32[]{:S(2)}) %collective-permute-start.20) | collective-permute-done | bytes 160 | tf_op jit(solution)/shard_map/ppermute | solution.py:160
  (85 shorter events, 10.8 us)
Async XLA Ops:
  6.7 15.0 %collective-permute-start.1 = (bf16[32,4096]{1,0:T(8,128)(2,1)}, bf16[32,4096]{1,0:T(8,128)(2,1)S(1)}, u32[]{:S(2)}, u32[]{:S(2)}) collective-permute-start(bf16[32,4096]{1,0:T(8,128)(2,1)} %get-tuple-element.16), channel_id=1, source_target_pairs={{0,2},{2,0},{4,6},{6,4},{8,10},{10,8},{12,14},{14,12},{1,3},{3,1},... | collective-permute-start | bytes 786440 | tf_op jit(solution)/shard_map/ppermute | solution.py:148
  9.7 15.7 %collective-permute-start.4 = (bf16[32,4096]{1,0:T(8,128)(2,1)}, bf16[32,4096]{1,0:T(8,128)(2,1)S(1)}, u32[]{:S(2)}, u32[]{:S(2)}) collective-permute-start(bf16[32,4096]{1,0:T(8,128)(2,1)} %get-tuple-element.17), channel_id=1, source_target_pairs={{0,4},{2,6},{4,0},{6,2},{8,12},{10,14},{12,8},{14,10},{1,5},{3,7},... | collective-permute-start | bytes 786440 | tf_op jit(solution)/shard_map/ppermute | solution.py:148
  11.3 10.5 %copy-start.18 = (bf16[32,4096]{1,0:T(8,128)(2,1)S(1)}, bf16[32,4096]{1,0:T(8,128)(2,1)}, u32[]{:S(2)}) copy-start(bf16[32,4096]{1,0:T(8,128)(2,1)} %get-tuple-element.21) | copy-start | bytes 786436
  11.3 14.1 %copy-start.17 = (bf16[32,4096]{1,0:T(8,128)(2,1)S(1)}, bf16[32,4096]{1,0:T(8,128)(2,1)}, u32[]{:S(2)}) copy-start(bf16[32,4096]{1,0:T(8,128)(2,1)} %get-tuple-element.22) | copy-start | bytes 786436
  17.3 3.1 %collective-permute-start = (f32[1,32]{1,0:T(1,128)S(1)}, f32[1,32]{1,0:T(1,128)S(1)}, u32[]{:S(2)}, u32[]{:S(2)}) collective-permute-start(f32[1,32]{1,0:T(1,128)S(1)} %bitcast.37), channel_id=1, source_target_pairs={{0,1},{1,0},{2,3},{3,2},{4,5},{5,4},{6,7},{7,6},{8,9},{9,8},{10,11... | collective-permute-start | bytes 392 | tf_op jit(solution)/shard_map/ppermute | solution.py:160
  17.3 19.0 %collective-permute-start.7 = (bf16[32,4096]{1,0:T(8,128)(2,1)S(1)}, bf16[32,4096]{1,0:T(8,128)(2,1)S(1)}, u32[]{:S(2)}, u32[]{:S(2)}) collective-permute-start(bf16[32,4096]{1,0:T(8,128)(2,1)S(1)} %copy-done.21), channel_id=1, source_target_pairs={{0,6},{2,4},{4,2},{6,0},{8,14},{10,12},{12,10},{14,8},{1,7},{3,5},... | collective-permute-start | bytes 786440 | tf_op jit(solution)/shard_map/ppermute | solution.py:148
  17.3 25.0 %collective-permute-start.10 = (bf16[32,4096]{1,0:T(8,128)(2,1)S(1)}, bf16[32,4096]{1,0:T(8,128)(2,1)S(1)}, u32[]{:S(2)}, u32[]{:S(2)}) collective-permute-start(bf16[32,4096]{1,0:T(8,128)(2,1)S(1)} %copy-done.20), channel_id=1, source_target_pairs={{0,8},{2,10},{4,12},{6,14},{8,0},{10,2},{12,4},{14,6},{1,9},{3,11}... | collective-permute-start | bytes 786440 | tf_op jit(solution)/shard_map/ppermute | solution.py:148
  20.4 36.4 %collective-permute-start.13 = (bf16[32,4096]{1,0:T(8,128)(2,1)S(1)}, bf16[32,4096]{1,0:T(8,128)(2,1)S(1)}, u32[]{:S(2)}, u32[]{:S(2)}) collective-permute-start(bf16[32,4096]{1,0:T(8,128)(2,1)S(1)} %copy-done.19), channel_id=1, source_target_pairs={{0,10},{2,8},{4,14},{6,12},{8,2},{10,0},{12,6},{14,4},{1,11},{3,9}... | collective-permute-start | bytes 786440 | tf_op jit(solution)/shard_map/ppermute | solution.py:148
  21.8 41.0 %collective-permute-start.16 = (bf16[32,4096]{1,0:T(8,128)(2,1)S(1)}, bf16[32,4096]{1,0:T(8,128)(2,1)S(1)}, u32[]{:S(2)}, u32[]{:S(2)}) collective-permute-start(bf16[32,4096]{1,0:T(8,128)(2,1)S(1)} %copy-done.18), channel_id=1, source_target_pairs={{0,12},{2,14},{4,8},{6,10},{8,4},{10,6},{12,0},{14,2},{1,13},{3,15... | collective-permute-start | bytes 786440 | tf_op jit(solution)/shard_map/ppermute | solution.py:148
  25.4 43.6 %collective-permute-start.19 = (bf16[32,4096]{1,0:T(8,128)(2,1)S(1)}, bf16[32,4096]{1,0:T(8,128)(2,1)S(1)}, u32[]{:S(2)}, u32[]{:S(2)}) collective-permute-start(bf16[32,4096]{1,0:T(8,128)(2,1)S(1)} %copy-done.17), channel_id=1, source_target_pairs={{0,14},{2,12},{4,10},{6,8},{8,6},{10,4},{12,2},{14,0},{1,15},{3,13... | collective-permute-start | bytes 786440 | tf_op jit(solution)/shard_map/ppermute | solution.py:148
  36.9 39.4 %collective-permute-start.3 = (f32[1,32]{1,0:T(1,128)S(1)}, f32[1,32]{1,0:T(1,128)S(1)}, u32[]{:S(2)}, u32[]{:S(2)}) collective-permute-start(f32[1,32]{1,0:T(1,128)S(1)} %bitcast.35), channel_id=1, source_target_pairs={{0,3},{1,2},{2,1},{3,0},{4,7},{5,6},{6,5},{7,4},{8,11},{9,10},{10,... | collective-permute-start | bytes 392 | tf_op jit(solution)/shard_map/ppermute | solution.py:160
  42.3 35.9 %collective-permute-start.2 = (f32[1,32]{1,0:T(1,128)S(1)}, f32[1,32]{1,0:T(1,128)S(1)}, u32[]{:S(2)}, u32[]{:S(2)}) collective-permute-start(f32[1,32]{1,0:T(1,128)S(1)} %bitcast.36), channel_id=1, source_target_pairs={{0,2},{1,3},{2,0},{3,1},{4,6},{5,7},{6,4},{7,5},{8,10},{9,11},{10,... | collective-permute-start | bytes 392 | tf_op jit(solution)/shard_map/ppermute | solution.py:160
  56.8 23.9 %collective-permute-start.6 = (f32[1,32]{1,0:T(1,128)S(1)}, f32[1,32]{1,0:T(1,128)S(1)}, u32[]{:S(2)}, u32[]{:S(2)}) collective-permute-start(f32[1,32]{1,0:T(1,128)S(1)} %bitcast.33), channel_id=1, source_target_pairs={{0,5},{1,4},{2,7},{3,6},{4,1},{5,0},{6,3},{7,2},{8,13},{9,12},{10,... | collective-permute-start | bytes 392 | tf_op jit(solution)/shard_map/ppermute | solution.py:160
  62.7 18.9 %collective-permute-start.5 = (f32[1,32]{1,0:T(1,128)S(1)}, f32[1,32]{1,0:T(1,128)S(1)}, u32[]{:S(2)}, u32[]{:S(2)}) collective-permute-start(f32[1,32]{1,0:T(1,128)S(1)} %bitcast.34), channel_id=1, source_target_pairs={{0,4},{1,5},{2,6},{3,7},{4,0},{5,1},{6,2},{7,3},{8,12},{9,13},{10,... | collective-permute-start | bytes 392 | tf_op jit(solution)/shard_map/ppermute | solution.py:160
  69.7 14.4 %collective-permute-start.9 = (f32[1,32]{1,0:T(1,128)S(1)}, f32[1,32]{1,0:T(1,128)S(1)}, u32[]{:S(2)}, u32[]{:S(2)}) collective-permute-start(f32[1,32]{1,0:T(1,128)S(1)} %bitcast.31), channel_id=1, source_target_pairs={{0,7},{1,6},{2,5},{3,4},{4,3},{5,2},{6,1},{7,0},{8,15},{9,14},{10,... | collective-permute-start | bytes 392 | tf_op jit(solution)/shard_map/ppermute | solution.py:160
  76.4 9.4 %collective-permute-start.8 = (f32[1,32]{1,0:T(1,128)S(1)}, f32[1,32]{1,0:T(1,128)S(1)}, u32[]{:S(2)}, u32[]{:S(2)}) collective-permute-start(f32[1,32]{1,0:T(1,128)S(1)} %bitcast.32), channel_id=1, source_target_pairs={{0,6},{1,7},{2,4},{3,5},{4,2},{5,3},{6,0},{7,1},{8,14},{9,15},{10,... | collective-permute-start | bytes 392 | tf_op jit(solution)/shard_map/ppermute | solution.py:160
  78.1 8.9 %collective-permute-start.12 = (f32[1,32]{1,0:T(1,128)S(1)}, f32[1,32]{1,0:T(1,128)S(1)}, u32[]{:S(2)}, u32[]{:S(2)}) collective-permute-start(f32[1,32]{1,0:T(1,128)S(1)} %bitcast.29), channel_id=1, source_target_pairs={{0,9},{1,8},{2,11},{3,10},{4,13},{5,12},{6,15},{7,14},{8,1},{9,0},... | collective-permute-start | bytes 392 | tf_op jit(solution)/shard_map/ppermute | solution.py:160
  80.7 8.2 %collective-permute-start.11 = (f32[1,32]{1,0:T(1,128)S(1)}, f32[1,32]{1,0:T(1,128)S(1)}, u32[]{:S(2)}, u32[]{:S(2)}) collective-permute-start(f32[1,32]{1,0:T(1,128)S(1)} %bitcast.30), channel_id=1, source_target_pairs={{0,8},{1,9},{2,10},{3,11},{4,12},{5,13},{6,14},{7,15},{8,0},{9,1},... | collective-permute-start | bytes 392 | tf_op jit(solution)/shard_map/ppermute | solution.py:160
  81.6 10.3 %collective-permute-start.15 = (f32[1,32]{1,0:T(1,128)S(1)}, f32[1,32]{1,0:T(1,128)S(1)}, u32[]{:S(2)}, u32[]{:S(2)}) collective-permute-start(f32[1,32]{1,0:T(1,128)S(1)} %bitcast.23), channel_id=1, source_target_pairs={{0,11},{1,10},{2,9},{3,8},{4,15},{5,14},{6,13},{7,12},{8,3},{9,2},... | collective-permute-start | bytes 392 | tf_op jit(solution)/shard_map/ppermute | solution.py:160
  84.1 9.8 %collective-permute-start.14 = (f32[1,32]{1,0:T(1,128)S(1)}, f32[1,32]{1,0:T(1,128)S(1)}, u32[]{:S(2)}, u32[]{:S(2)}) collective-permute-start(f32[1,32]{1,0:T(1,128)S(1)} %bitcast.24), channel_id=1, source_target_pairs={{0,10},{1,11},{2,8},{3,9},{4,14},{5,15},{6,12},{7,13},{8,2},{9,3},... | collective-permute-start | bytes 392 | tf_op jit(solution)/shard_map/ppermute | solution.py:160
  85.8 8.1 %collective-permute-start.18 = (f32[1,32]{1,0:T(1,128)S(1)}, f32[1,32]{1,0:T(1,128)S(1)}, u32[]{:S(2)}, u32[]{:S(2)}) collective-permute-start(f32[1,32]{1,0:T(1,128)S(1)} %bitcast.25), channel_id=1, source_target_pairs={{0,13},{1,12},{2,15},{3,14},{4,9},{5,8},{6,11},{7,10},{8,5},{9,4},... | collective-permute-start | bytes 392 | tf_op jit(solution)/shard_map/ppermute | solution.py:160
  87.1 6.8 %collective-permute-start.17 = (f32[1,32]{1,0:T(1,128)S(1)}, f32[1,32]{1,0:T(1,128)S(1)}, u32[]{:S(2)}, u32[]{:S(2)}) collective-permute-start(f32[1,32]{1,0:T(1,128)S(1)} %bitcast.26), channel_id=1, source_target_pairs={{0,12},{1,13},{2,14},{3,15},{4,8},{5,9},{6,10},{7,11},{8,4},{9,5},... | collective-permute-start | bytes 392 | tf_op jit(solution)/shard_map/ppermute | solution.py:160
  88.9 5.7 %collective-permute-start.21 = (f32[1,32]{1,0:T(1,128)S(1)}, f32[1,32]{1,0:T(1,128)S(1)}, u32[]{:S(2)}, u32[]{:S(2)}) collective-permute-start(f32[1,32]{1,0:T(1,128)S(1)} %bitcast.27), channel_id=1, source_target_pairs={{0,15},{1,14},{2,13},{3,12},{4,11},{5,10},{6,9},{7,8},{8,7},{9,6},... | collective-permute-start | bytes 392 | tf_op jit(solution)/shard_map/ppermute | solution.py:160
  91.9 6.2 %collective-permute-start.20 = (f32[1,32]{1,0:T(1,128)S(1)}, f32[1,32]{1,0:T(1,128)S(1)}, u32[]{:S(2)}, u32[]{:S(2)}) collective-permute-start(f32[1,32]{1,0:T(1,128)S(1)} %bitcast.28), channel_id=1, source_target_pairs={{0,14},{1,15},{2,12},{3,13},{4,10},{5,11},{6,8},{7,9},{8,6},{9,7},... | collective-permute-start | bytes 392 | tf_op jit(solution)/shard_map/ppermute | solution.py:160
  (20 other events, 62.7 us)

commit v2 on v0

v2 whole, which is shorter than its diff:
```python
import functools
import math

import jax
import jax.numpy as jnp
from jax import lax
from jax.experimental import pallas as pl
from jax.experimental.pallas import tpu as pltpu
from jax.sharding import PartitionSpec as P

HD = 128
SCALE = math.log2(math.e) / math.sqrt(HD)
MAX_PAIRWISE = 16


def route_kernel(capacity, by_xor, owner_ref, prompt_ref, query_ref, column_ref, *refs):
    *out_refs, picks_ref = refs
    tok_rows = prompt_ref.shape[1]
    peers = picks_ref.shape[0] // capacity

    @pl.when(pl.program_id(0) == 0)
    def _():
        prompt = prompt_ref[...]
        target = lax.fori_loop(
            0,
            owner_ref.shape[0],
            lambda k, t: jnp.where(prompt == k, owner_ref[k], t),
            jnp.zeros_like(prompt),
            unroll=owner_ref.shape[0] <= MAX_PAIRWISE,
        )
        peer_row = lax.broadcasted_iota(jnp.int32, (peers, tok_rows), 0)
        hits = (target == peer_row).astype(jnp.float32)
        earlier_mask = lax.broadcasted_iota(jnp.int32, (tok_rows, tok_rows), 0) < (
            lax.broadcasted_iota(jnp.int32, (tok_rows, tok_rows), 1)
        )
        earlier = jnp.dot(
            hits.astype(jnp.bfloat16),
            earlier_mask.astype(jnp.bfloat16),
            preferred_element_type=jnp.float32,
        )
        rank = jnp.sum(earlier * hits, axis=0, keepdims=True).astype(jnp.int32)
        place = target ^ lax.axis_index("dp") if by_xor else target
        column = place * capacity + rank
        column_ref[...] = column
        slot_row = lax.broadcasted_iota(jnp.int32, picks_ref.shape, 0)
        picks_ref[...] = (column == slot_row).astype(jnp.bfloat16)

    for n, out_ref in enumerate(out_refs):
        rows = out_ref.shape[0]
        out_ref[...] = jnp.dot(
            picks_ref[n * rows : (n + 1) * rows], query_ref[...], preferred_element_type=jnp.float32
        ).astype(jnp.bfloat16)


def route(queries, answer_prompt, prompt_owner, peers, capacity, by_xor):
    tok_rows, width = queries.shape
    pieces = peers if by_xor else 1
    piece_rows = peers * capacity // pieces
    step = min(width, 1024)
    return pl.pallas_call(
        functools.partial(route_kernel, capacity, by_xor),
        grid=(width // step,),
        in_specs=[
            pl.BlockSpec(memory_space=pltpu.SMEM),
            pl.BlockSpec((1, tok_rows), lambda c: (0, 0)),
            pl.BlockSpec((tok_rows, step), lambda c: (0, c)),
        ],
        out_specs=[pl.BlockSpec((1, tok_rows), lambda c: (0, 0))]
        + [pl.BlockSpec((piece_rows, step), lambda c: (0, c))] * pieces,
        out_shape=[jax.ShapeDtypeStruct((1, tok_rows), jnp.int32)]
        + [jax.ShapeDtypeStruct((piece_rows, width), jnp.bfloat16)] * pieces,
        scratch_shapes=[pltpu.VMEM((peers * capacity, tok_rows), jnp.bfloat16)],
        name="route",
    )(prompt_owner, answer_prompt.reshape(1, tok_rows), queries)


def attend_block(query_ref, key_ref, value_ref, weight_ref, shift_by_peak):
    rows = query_ref.shape[0]
    kv_local = key_ref.shape[1] // HD
    group_size = query_ref.shape[1] // key_ref.shape[1]
    total = jnp.zeros((rows, HD), jnp.float32)
    smallest = largest = None
    for g in range(kv_local):
        heads = [slice((g * group_size + h) * HD, (g * group_size + h + 1) * HD) for h in range(group_size)]
        kv = slice(g * HD, (g + 1) * HD)
        stacked = jnp.concatenate([query_ref[:, head] for head in heads], axis=0)
        logits = lax.dot_general(
            stacked, key_ref[:, kv], (((1,), (1,)), ((), ())), preferred_element_type=jnp.float32
        )
        if shift_by_peak:
            logits = logits - jnp.max(logits, axis=1, keepdims=True)
        exponent = jnp.exp2(logits * SCALE)
        norm = jnp.sum(exponent, axis=1, keepdims=True)
        smallest = norm if g == 0 else jnp.minimum(smallest, norm)
        largest = norm if g == 0 else jnp.maximum(largest, norm)
        probs = (exponent * (1.0 / norm)).astype(jnp.bfloat16)
        attended = jnp.dot(probs, value_ref[:, kv], preferred_element_type=jnp.float32)
        attended = attended.astype(jnp.bfloat16).astype(jnp.float32)
        for h, head in enumerate(heads):
            total += attended[h * rows : (h + 1) * rows] * weight_ref[:, head]
    return jnp.sum(total.T, axis=0, keepdims=True), jnp.min(smallest), jnp.max(largest)


def attend_kernel(query_ref, key_ref, value_ref, weight_ref, score_ref):
    score, smallest, largest = attend_block(query_ref, key_ref, value_ref, weight_ref, False)
    score_ref[0] = score

    @pl.when(jnp.logical_not((smallest > 1e-25) & (largest < 1e25)))
    def _():
        score_ref[0] = attend_block(query_ref, key_ref, value_ref, weight_ref, True)[0]


def attend_score(query_rows, key_rows, value_rows, score_weight):
    row_count, width = query_rows.shape
    context_len, kv_width = key_rows.shape
    block = math.gcd(row_count, 32)
    blocks = row_count // block
    return pl.pallas_call(
        attend_kernel,
        grid=(blocks,),
        in_specs=[pl.BlockSpec((block, width), lambda r: (r, 0))]
        + [pl.BlockSpec(memory_space=pltpu.VMEM)] * 3,
        out_specs=pl.BlockSpec((1, 1, block), lambda r: (r, 0, 0)),
        out_shape=jax.ShapeDtypeStruct((blocks, 1, block), jnp.float32),
        compiler_params=pltpu.CompilerParams(vmem_limit_bytes=24 << 20),
        cost_estimate=pl.CostEstimate(
            flops=4 * row_count * width * context_len,
            bytes_accessed=2 * (row_count * width + 2 * context_len * kv_width),
            transcendentals=row_count * width // HD * context_len,
        ),
        name="attend_score",
    )(query_rows, key_rows, value_rows, score_weight.reshape(1, -1)).reshape(1, row_count)


def pick_slots(returned, column):
    slots = lax.broadcasted_iota(jnp.int32, (column.shape[1], returned.shape[1]), 1)
    return jnp.sum(jnp.where(column.reshape(-1, 1) == slots, returned, 0.0), axis=1)


def on_device(queries, answer_prompt, prompt_owner, context_keys, context_values, score_weight):
    tok_rows, width = queries.shape
    peers = lax.axis_size("dp")
    cores = lax.axis_size("tensor")
    capacity = max(2, 2 * tok_rows // peers)
    by_xor = peers <= MAX_PAIRWISE and peers & (peers - 1) == 0 and capacity % 16 == 0
    column, *pieces = route(
        queries, answer_prompt, prompt_owner, peers, capacity, by_xor
    )
    score = functools.partial(
        attend_score,
        key_rows=context_keys,
        value_rows=context_values,
        score_weight=score_weight,
    )
    if by_xor:
        pairs = [[(k, k ^ s) for k in range(peers)] for s in range(peers)]
        arrived = [pieces[0]] + [lax.ppermute(pieces[s], "dp", pairs[s]) for s in range(1, peers)]
        arrived[0], arrived[1] = lax.optimization_barrier((arrived[0], arrived[1]))
        returned = [score(arrived[0])]
        for s in range(1, peers):
            returned.append(lax.ppermute(score(arrived[s]), "dp", pairs[s]))
        own = pick_slots(jnp.concatenate(returned, axis=1), column)
        other = lax.ppermute(own, "tensor", [(k, (k + 1) % cores) for k in range(cores)])
        return own + other
    arrived = lax.all_to_all(
        pieces[0].reshape(peers, capacity, width), "dp", split_axis=0, concat_axis=0, tiled=True
    )
    own = score(arrived.reshape(peers * capacity, width))
    returned = lax.all_to_all(
        own.reshape(peers, capacity), "dp", split_axis=0, concat_axis=0, tiled=True
    )
    head_terms = pick_slots(returned.reshape(1, peers * capacity), column)
    return lax.psum(head_terms, "tensor")


def solution(mesh):
    return jax.shard_map(
        on_device,
        mesh=mesh,
        in_specs=(
            P(("groups", "dp"), "tensor"),
            P(("groups", "dp"), None),
            P("groups"),
            P(("groups", "dp"), "tensor"),
            P(("groups", "dp"), "tensor"),
            P("tensor"),
        ),
        out_specs=P(("groups", "dp")),
        check_vma=False,
    )
```

time: 150 us -> 75.1 us (0.50)
  waiting for transfers between devices: 92.9 us -> 19.3 us
  Pallas kernels: 0 us -> 32.5 us
  matrix products: 21.2 us -> 0 us
  local copies, waits for them, and re-layouts: 14.4 us -> 2.94 us
  starting transfers between devices: 10.9 us -> 19.6 us
  other arithmetic: 7.21 us -> 0.68 us
  blocking collectives: 2.97 us -> 0 us
    all_to_all x2 -> x0, waiting for transfers between devices: 92.9 us -> none  [the longest x1 48.4 us: on_device(): lax.all_to_all(attended.reshape(sources, slot_items, feature_width), 'dp'...]
    pallas_call x0 -> x9, Pallas kernels: none -> 32.5 us  [the longest x8 28.1 us: attend_score(): pl.pallas_call(attend_kernel, grid=(blocks,), in_specs=[pl.BlockSpec((blo...]
    dot_general x8 -> x0, matrix products: 21.2 us -> none  [the longest x4 16 us: per_head(): jnp.dot(weights, packed[2], preferred_element_type=jnp.float32)]
    ppermute x0 -> x15, starting transfers between devices: none -> 19.6 us  [the longest x7 13.8 us: on_device(): lax.ppermute(pieces[s], 'dp', pairs[s])]
    ppermute x0 -> x15, waiting for transfers between devices: none -> 19.3 us  [the longest x7 13.5 us: on_device(): lax.ppermute(pieces[s], 'dp', pairs[s])]
    all_to_all x2 -> x0, starting transfers between devices: 10.9 us -> none  [the longest x1 7.25 us: on_device(): lax.all_to_all(outgoing, 'dp', split_axis=0, concat_axis=0, tiled=True)]
    reduce_sum x7 -> x1, other arithmetic: 6.93 us -> 0.17 us  [pick_slots(): jnp.sum(jnp.where(column.reshape(-1, 1) == slots, returned, 0.0), axis=1)]
    scatter x1 -> x0, local copies, waits for them, and re-layouts: 4.29 us -> none  [on_device(): jnp.zeros((peer_count * capacity, feature_width), jnp.bfloat16)]
  transfers between devices with their start and end apart: 2 -> 15, of which waited for: 2 -> 6; matrix products, arithmetic and copies ran while one was open for 3% -> 0% of each run, Pallas kernels for 0% -> 37%
where the time goes in v2:
time: 75.1 us
  Pallas kernels  32.5 us (43%)
  starting transfers between devices  19.6 us (26%)
  waiting for transfers between devices  19.3 us (26%)
  local copies, waits for them, and re-layouts  2.94 us (4%)
    pallas_call x8, Pallas kernels, attend_score(): pl.pallas_call(attend_kernel, grid=(blocks,), in_specs=[pl.BlockSpec((blo...  28.1 us
    ppermute x7, starting transfers between devices, on_device(): lax.ppermute(pieces[s], 'dp', pairs[s])  13.8 us
    ppermute x7, waiting for transfers between devices, on_device(): lax.ppermute(pieces[s], 'dp', pairs[s])  13.5 us
    ppermute x7, starting transfers between devices, on_device(): returned.append(lax.ppermute(score(arrived[s]), 'dp', pairs[s]))  5.72 us
    ppermute x7, waiting for transfers between devices, on_device(): returned.append(lax.ppermute(score(arrived[s]), 'dp', pairs[s]))  4.64 us
    pallas_call x1, Pallas kernels, route(): pl.pallas_call(functools.partial(route_kernel, capacity, by_xor), grid=(w...  4.33 us
    unnamed x12, local copies, waits for them, and re-layouts  2.84 us
  transfers between devices with their start and end apart: 15, of which 6 were waited for; matrix products, arithmetic and copies ran while one was open for 0% of the time, Pallas kernels for 37%

profile of v2, /device:TPU:0, one launch (start us, length us, event | category | flops | bytes accessed | tf_op | source)
XLA Modules:
  0.0 75.1 jit_solution(516068735483958733)
XLA Ops:
  0.0 4.3 %route.1 = (s32[1,128]{1,0:T(1,128)}, bf16[32,4096]{1,0:T(8,128)(2,1)}, bf16[32,4096]{1,0:T(8,128)(2,1)}, bf16[32,4096]{1,0:T(8,128)(2,1)}, bf16[32,4096]{1,0:T(...) custom-call(s32[8]{0:T(128)} %owner_ref.1, ...), custom_call_target="tpu_custom_call" | custom-call | tf_op jit(solution)/shard_map/route/pallas_call | solution.py:60
  4.3 3.0 %collective-permute-start = (bf16[32,4096]{1,0:T(8,128)(2,1)}, bf16[32,4096]{1,0:T(8,128)(2,1)S(1)}, u32[]{:S(2)}, u32[]{:S(2)}) collective-permute-start(bf16[32,4096]{1,0:T(8,128)(2,1)} %get-tuple-element.18), channel_id=1, source_target_pairs={{0,2},{2,0},{4,6},{6,4},{8,10},{10,8},{12,14},{14,12},{1,3},{3,1},... | collective-permute-start | bytes 786440 | tf_op jit(solution)/shard_map/ppermute | solution.py:157
  7.3 1.6 %collective-permute-start.2 = (bf16[32,4096]{1,0:T(8,128)(2,1)}, bf16[32,4096]{1,0:T(8,128)(2,1)S(1)}, u32[]{:S(2)}, u32[]{:S(2)}) collective-permute-start(bf16[32,4096]{1,0:T(8,128)(2,1)} %get-tuple-element.21), channel_id=1, source_target_pairs={{0,4},{2,6},{4,0},{6,2},{8,12},{10,14},{12,8},{14,10},{1,5},{3,7},... | collective-permute-start | bytes 786440 | tf_op jit(solution)/shard_map/ppermute | solution.py:157
  8.9 3.0 %collective-permute-start.6 = (bf16[32,4096]{1,0:T(8,128)(2,1)}, bf16[32,4096]{1,0:T(8,128)(2,1)S(1)}, u32[]{:S(2)}, u32[]{:S(2)}) collective-permute-start(bf16[32,4096]{1,0:T(8,128)(2,1)} %get-tuple-element.23), channel_id=1, source_target_pairs={{0,8},{2,10},{4,12},{6,14},{8,0},{10,2},{12,4},{14,6},{1,9},{3,11}... | collective-permute-start | bytes 786440 | tf_op jit(solution)/shard_map/ppermute | solution.py:157
  11.9 1.3 %collective-permute-start.8 = (bf16[32,4096]{1,0:T(8,128)(2,1)}, bf16[32,4096]{1,0:T(8,128)(2,1)S(1)}, u32[]{:S(2)}, u32[]{:S(2)}) collective-permute-start(bf16[32,4096]{1,0:T(8,128)(2,1)} %get-tuple-element.24), channel_id=1, source_target_pairs={{0,10},{2,8},{4,14},{6,12},{8,2},{10,0},{12,6},{14,4},{1,11},{3,9}... | collective-permute-start | bytes 786440 | tf_op jit(solution)/shard_map/ppermute | solution.py:157
  13.8 3.8 %collective-permute-start.10 = (bf16[32,4096]{1,0:T(8,128)(2,1)}, bf16[32,4096]{1,0:T(8,128)(2,1)S(1)}, u32[]{:S(2)}, u32[]{:S(2)}) collective-permute-start(bf16[32,4096]{1,0:T(8,128)(2,1)} %get-tuple-element.25), channel_id=1, source_target_pairs={{0,12},{2,14},{4,8},{6,10},{8,4},{10,6},{12,0},{14,2},{1,13},{3,15... | collective-permute-start | bytes 786440 | tf_op jit(solution)/shard_map/ppermute | solution.py:157
  17.7 1.2 %copy-done.1 = bf16[1024,512]{1,0:T(8,128)(2,1)S(1)} copy-done((bf16[1024,512]{1,0:T(8,128)(2,1)S(1)}, bf16[1024,512]{1,0:T(8,128)(2,1)}, u32[]{:S(2)}) %copy-start.1) | copy-done | bytes 1048600
  19.9 2.1 %attend_score.8 = f32[1,1,32]{2,1,0:T(1,128)S(1)} custom-call(bf16[32,4096]{1,0:T(8,128)(2,1)S(1)} %copy-done.3, bf16[1024,512]{1,0:T(8,128)(2,1)S(1)} %copy-done, bf16[1024,512]{1,0:T(8,128)(2,1)S(1)} %copy-done.1, f32[1,4096]{1,0:T(1,128)S(1)} %bitcast.12), custom_call_target="tpu_custom_call" | custom-call | flops 536870912 | bytes 2359296 | tf_op jit(solution)/shard_map/attend_score/pallas_call | solution.py:118
  22.0 5.1 %collective-permute-done.2.query_ref = bf16[32,4096]{1,0:T(8,128)(2,1)S(1)} collective-permute-done((bf16[32,4096]{1,0:T(8,128)(2,1)}, bf16[32,4096]{1,0:T(8,128)(2,1)S(1)}, u32[]{:S(2)}, u32[]{:S(2)}) %collective-permute-start.2) | collective-permute-done | bytes 262176 | tf_op jit(solution)/shard_map/ppermute | solution.py:157
  27.1 1.1 %collective-permute-start.12 = (bf16[32,4096]{1,0:T(8,128)(2,1)S(1)}, bf16[32,4096]{1,0:T(8,128)(2,1)S(1)}, u32[]{:S(2)}, u32[]{:S(2)}) collective-permute-start(bf16[32,4096]{1,0:T(8,128)(2,1)S(1)} %copy-done.5), channel_id=1, source_target_pairs={{0,14},{2,12},{4,10},{6,8},{8,6},{10,4},{12,2},{14,0},{1,15},{3,13... | collective-permute-start | bytes 786440 | tf_op jit(solution)/shard_map/ppermute | solution.py:157
  28.1 4.8 %attend_score.9 = f32[1,1,32]{2,1,0:T(1,128)S(1)} custom-call(bf16[32,4096]{1,0:T(8,128)(2,1)S(1)} %collective-permute-done.query_ref, bf16[1024,512]{1,0:T(8,128)(2,1)S(1)} %copy-done, bf16[1024,512]{1,0:T(8,128)(2,1)S(1)} %copy-done.1, f32[1,4096]{1,0:T(1,128)S(1)} %bitcast.13), custom_call_target="tpu_custom_call" | custom-call | flops 536870912 | bytes 2359296 | tf_op jit(solution)/shard_map/attend_score/pallas_call | solution.py:118
  32.9 2.3 %attend_score.10 = f32[1,1,32]{2,1,0:T(1,128)S(1)} custom-call(bf16[32,4096]{1,0:T(8,128)(2,1)S(1)} %collective-permute-done.2.query_ref, bf16[1024,512]{1,0:T(8,128)(2,1)S(1)} %copy-done, bf16[1024,512]{1,0:T(8,128)(2,1)S(1)} %copy-done.1, f32[1,4096]{1,0:T(1,128)S(1)} %bitcast.14), custom_call_target="tpu_custom_call" | custom-call | flops 536870912 | bytes 2359296 | tf_op jit(solution)/shard_map/attend_score/pallas_call | solution.py:118
  35.3 2.1 %attend_score.11 = f32[1,1,32]{2,1,0:T(1,128)S(1)} custom-call(bf16[32,4096]{1,0:T(8,128)(2,1)S(1)} %collective-permute-done.4.query_ref, bf16[1024,512]{1,0:T(8,128)(2,1)S(1)} %copy-done, bf16[1024,512]{1,0:T(8,128)(2,1)S(1)} %copy-done.1, f32[1,4096]{1,0:T(1,128)S(1)} %bitcast.15), custom_call_target="tpu_custom_call" | custom-call | flops 536870912 | bytes 2359296 | tf_op jit(solution)/shard_map/attend_score/pallas_call | solution.py:118
  37.4 1.3 %collective-permute-start.3 = (f32[1,32]{1,0:T(1,128)S(1)}, f32[1,32]{1,0:T(1,128)S(1)}, u32[]{:S(2)}, u32[]{:S(2)}) collective-permute-start(f32[1,32]{1,0:T(1,128)S(1)} %bitcast.21), channel_id=1, source_target_pairs={{0,4},{2,6},{4,0},{6,2},{8,12},{10,14},{12,8},{14,10},{1,5},{3,7},... | collective-permute-start | bytes 392 | tf_op jit(solution)/shard_map/ppermute | solution.py:161
  38.6 2.3 %attend_score.12 = f32[1,1,32]{2,1,0:T(1,128)S(1)} custom-call(bf16[32,4096]{1,0:T(8,128)(2,1)S(1)} %collective-permute-done.6.query_ref, bf16[1024,512]{1,0:T(8,128)(2,1)S(1)} %copy-done, bf16[1024,512]{1,0:T(8,128)(2,1)S(1)} %copy-done.1, f32[1,4096]{1,0:T(1,128)S(1)} %bitcast.16), custom_call_target="tpu_custom_call" | custom-call | flops 536870912 | bytes 2359296 | tf_op jit(solution)/shard_map/attend_score/pallas_call | solution.py:118
  40.9 7.8 %collective-permute-done.8.query_ref = bf16[32,4096]{1,0:T(8,128)(2,1)S(1)} collective-permute-done((bf16[32,4096]{1,0:T(8,128)(2,1)}, bf16[32,4096]{1,0:T(8,128)(2,1)S(1)}, u32[]{:S(2)}, u32[]{:S(2)}) %collective-permute-start.8) | collective-permute-done | bytes 262176 | tf_op jit(solution)/shard_map/ppermute | solution.py:157
  49.6 4.8 %attend_score.13 = f32[1,1,32]{2,1,0:T(1,128)S(1)} custom-call(bf16[32,4096]{1,0:T(8,128)(2,1)S(1)} %collective-permute-done.8.query_ref, bf16[1024,512]{1,0:T(8,128)(2,1)S(1)} %copy-done, bf16[1024,512]{1,0:T(8,128)(2,1)S(1)} %copy-done.1, f32[1,4096]{1,0:T(1,128)S(1)} %bitcast.17), custom_call_target="tpu_custom_call" | custom-call | flops 536870912 | bytes 2359296 | tf_op jit(solution)/shard_map/attend_score/pallas_call | solution.py:118
  54.4 1.7 %collective-permute-start.7 = (f32[1,32]{1,0:T(1,128)S(1)}, f32[1,32]{1,0:T(1,128)S(1)}, u32[]{:S(2)}, u32[]{:S(2)}) collective-permute-start(f32[1,32]{1,0:T(1,128)S(1)} %bitcast.24), channel_id=1, source_target_pairs={{0,8},{2,10},{4,12},{6,14},{8,0},{10,2},{12,4},{14,6},{1,9},{3,11}... | collective-permute-start | bytes 392 | tf_op jit(solution)/shard_map/ppermute | solution.py:161
  56.1 4.8 %attend_score.14 = f32[1,1,32]{2,1,0:T(1,128)S(1)} custom-call(bf16[32,4096]{1,0:T(8,128)(2,1)S(1)} %collective-permute-done.10.query_ref, bf16[1024,512]{1,0:T(8,128)(2,1)S(1)} %copy-done, bf16[1024,512]{1,0:T(8,128)(2,1)S(1)} %copy-done.1, f32[1,4096]{1,0:T(1,128)S(1)} %bitcast.18), custom_call_target="tpu_custom_call" | custom-call | flops 536870912 | bytes 2359296 | tf_op jit(solution)/shard_map/attend_score/pallas_call | solution.py:118
  61.0 5.0 %attend_score.15 = f32[1,1,32]{2,1,0:T(1,128)S(1)} custom-call(bf16[32,4096]{1,0:T(8,128)(2,1)S(1)} %collective-permute-done.12.query_ref, bf16[1024,512]{1,0:T(8,128)(2,1)S(1)} %copy-done, bf16[1024,512]{1,0:T(8,128)(2,1)S(1)} %copy-done.1, f32[1,4096]{1,0:T(1,128)S(1)} %bitcast.19), custom_call_target="tpu_custom_call" | custom-call | flops 536870912 | bytes 2359296 | tf_op jit(solution)/shard_map/attend_score/pallas_call | solution.py:118
  66.1 1.7 %collective-permute-start.13 = (f32[1,32]{1,0:T(1,128)S(1)}, f32[1,32]{1,0:T(1,128)S(1)}, u32[]{:S(2)}, u32[]{:S(2)}) collective-permute-start(f32[1,32]{1,0:T(1,128)S(1)} %bitcast.27), channel_id=1, source_target_pairs={{0,14},{2,12},{4,10},{6,8},{8,6},{10,4},{12,2},{14,0},{1,15},{3,13... | collective-permute-start | bytes 392 | tf_op jit(solution)/shard_map/ppermute | solution.py:161
  67.8 3.6 %collective-permute-done.11 = f32[1,32]{1,0:T(1,128)S(1)} collective-permute-done((f32[1,32]{1,0:T(1,128)S(1)}, f32[1,32]{1,0:T(1,128)S(1)}, u32[]{:S(2)}, u32[]{:S(2)}) %collective-permute-start.11) | collective-permute-done | bytes 160 | tf_op jit(solution)/shard_map/ppermute | solution.py:161
  71.5 1.0 %collective-permute-done.13 = f32[1,32]{1,0:T(1,128)S(1)} collective-permute-done((f32[1,32]{1,0:T(1,128)S(1)}, f32[1,32]{1,0:T(1,128)S(1)}, u32[]{:S(2)}, u32[]{:S(2)}) %collective-permute-start.13) | collective-permute-done | bytes 160 | tf_op jit(solution)/shard_map/ppermute | solution.py:161
  73.5 1.1 %collective-permute-done.14 = f32[128]{0:T(128)S(1)} collective-permute-done((f32[128]{0:T(128)S(1)}, f32[128]{0:T(128)S(1)}, u32[]{:S(2)}, u32[]{:S(2)}) %collective-permute-start.14) | collective-permute-done | bytes 544 | tf_op jit(solution)/shard_map/ppermute | solution.py:163
  (30 shorter events, 4.3 us)
Async XLA Ops:
  0.0 17.7 %copy-start = (bf16[1024,512]{1,0:T(8,128)(2,1)S(1)}, bf16[1024,512]{1,0:T(8,128)(2,1)}, u32[]{:S(2)}) copy-start(bf16[1024,512]{1,0:T(8,128)(2,1)} %key_ref.15) | copy-start | bytes 3145732
  0.0 17.7 %copy-start.2 = (f32[4096]{0:T(1024)S(1)}, f32[4096]{0:T(1024)}, u32[]{:S(2)}) copy-start(f32[4096]{0:T(1024)} %param.11) | copy-start | bytes 49156
  4.3 9.5 %collective-permute-start = (bf16[32,4096]{1,0:T(8,128)(2,1)}, bf16[32,4096]{1,0:T(8,128)(2,1)S(1)}, u32[]{:S(2)}, u32[]{:S(2)}) collective-permute-start(bf16[32,4096]{1,0:T(8,128)(2,1)} %get-tuple-element.18), channel_id=1, source_target_pairs={{0,2},{2,0},{4,6},{6,4},{8,10},{10,8},{12,14},{14,12},{1,3},{3,1},... | collective-permute-start | bytes 786440 | tf_op jit(solution)/shard_map/ppermute | solution.py:157
  7.3 19.7 %collective-permute-start.2 = (bf16[32,4096]{1,0:T(8,128)(2,1)}, bf16[32,4096]{1,0:T(8,128)(2,1)S(1)}, u32[]{:S(2)}, u32[]{:S(2)}) collective-permute-start(bf16[32,4096]{1,0:T(8,128)(2,1)} %get-tuple-element.21), channel_id=1, source_target_pairs={{0,4},{2,6},{4,0},{6,2},{8,12},{10,14},{12,8},{14,10},{1,5},{3,7},... | collective-permute-start | bytes 786440 | tf_op jit(solution)/shard_map/ppermute | solution.py:157
  8.9 26.3 %collective-permute-start.4 = (bf16[32,4096]{1,0:T(8,128)(2,1)}, bf16[32,4096]{1,0:T(8,128)(2,1)S(1)}, u32[]{:S(2)}, u32[]{:S(2)}) collective-permute-start(bf16[32,4096]{1,0:T(8,128)(2,1)} %get-tuple-element.22), channel_id=1, source_target_pairs={{0,6},{2,4},{4,2},{6,0},{8,14},{10,12},{12,10},{14,8},{1,7},{3,5},... | collective-permute-start | bytes 786440 | tf_op jit(solution)/shard_map/ppermute | solution.py:157
  8.9 28.5 %collective-permute-start.6 = (bf16[32,4096]{1,0:T(8,128)(2,1)}, bf16[32,4096]{1,0:T(8,128)(2,1)S(1)}, u32[]{:S(2)}, u32[]{:S(2)}) collective-permute-start(bf16[32,4096]{1,0:T(8,128)(2,1)} %get-tuple-element.23), channel_id=1, source_target_pairs={{0,8},{2,10},{4,12},{6,14},{8,0},{10,2},{12,4},{14,6},{1,9},{3,11}... | collective-permute-start | bytes 786440 | tf_op jit(solution)/shard_map/ppermute | solution.py:157
  11.9 36.8 %collective-permute-start.8 = (bf16[32,4096]{1,0:T(8,128)(2,1)}, bf16[32,4096]{1,0:T(8,128)(2,1)S(1)}, u32[]{:S(2)}, u32[]{:S(2)}) collective-permute-start(bf16[32,4096]{1,0:T(8,128)(2,1)} %get-tuple-element.24), channel_id=1, source_target_pairs={{0,10},{2,8},{4,14},{6,12},{8,2},{10,0},{12,6},{14,4},{1,11},{3,9}... | collective-permute-start | bytes 786440 | tf_op jit(solution)/shard_map/ppermute | solution.py:157
  13.8 40.5 %collective-permute-start.10 = (bf16[32,4096]{1,0:T(8,128)(2,1)}, bf16[32,4096]{1,0:T(8,128)(2,1)S(1)}, u32[]{:S(2)}, u32[]{:S(2)}) collective-permute-start(bf16[32,4096]{1,0:T(8,128)(2,1)} %get-tuple-element.25), channel_id=1, source_target_pairs={{0,12},{2,14},{4,8},{6,10},{8,4},{10,6},{12,0},{14,2},{1,13},{3,15... | collective-permute-start | bytes 786440 | tf_op jit(solution)/shard_map/ppermute | solution.py:157
  17.7 1.2 %copy-start.1 = (bf16[1024,512]{1,0:T(8,128)(2,1)S(1)}, bf16[1024,512]{1,0:T(8,128)(2,1)}, u32[]{:S(2)}) copy-start(bf16[1024,512]{1,0:T(8,128)(2,1)} %value_ref.15) | copy-start | bytes 3145732
  18.9 0.9 %copy-start.3 = (bf16[32,4096]{1,0:T(8,128)(2,1)S(1)}, bf16[32,4096]{1,0:T(8,128)(2,1)}, u32[]{:S(2)}) copy-start(bf16[32,4096]{1,0:T(8,128)(2,1)} %get-tuple-element.19.query_ref) | copy-start | bytes 786436
  19.9 7.2 %copy-start.5 = (bf16[32,4096]{1,0:T(8,128)(2,1)S(1)}, bf16[32,4096]{1,0:T(8,128)(2,1)}, u32[]{:S(2)}) copy-start(bf16[32,4096]{1,0:T(8,128)(2,1)} %get-tuple-element.26) | copy-start | bytes 786436
  27.1 33.9 %collective-permute-start.12 = (bf16[32,4096]{1,0:T(8,128)(2,1)S(1)}, bf16[32,4096]{1,0:T(8,128)(2,1)S(1)}, u32[]{:S(2)}, u32[]{:S(2)}) collective-permute-start(bf16[32,4096]{1,0:T(8,128)(2,1)S(1)} %copy-done.5), channel_id=1, source_target_pairs={{0,14},{2,12},{4,10},{6,8},{8,6},{10,4},{12,2},{14,0},{1,15},{3,13... | collective-permute-start | bytes 786440 | tf_op jit(solution)/shard_map/ppermute | solution.py:157
  35.2 30.9 %collective-permute-start.1 = (f32[1,32]{1,0:T(1,128)S(1)}, f32[1,32]{1,0:T(1,128)S(1)}, u32[]{:S(2)}, u32[]{:S(2)}) collective-permute-start(f32[1,32]{1,0:T(1,128)S(1)} %bitcast.23), channel_id=1, source_target_pairs={{0,2},{2,0},{4,6},{6,4},{8,10},{10,8},{12,14},{14,12},{1,3},{3,1},... | collective-permute-start | bytes 392 | tf_op jit(solution)/shard_map/ppermute | solution.py:161
  37.4 28.8 %collective-permute-start.3 = (f32[1,32]{1,0:T(1,128)S(1)}, f32[1,32]{1,0:T(1,128)S(1)}, u32[]{:S(2)}, u32[]{:S(2)}) collective-permute-start(f32[1,32]{1,0:T(1,128)S(1)} %bitcast.21), channel_id=1, source_target_pairs={{0,4},{2,6},{4,0},{6,2},{8,12},{10,14},{12,8},{14,10},{1,5},{3,7},... | collective-permute-start | bytes 392 | tf_op jit(solution)/shard_map/ppermute | solution.py:161
  48.7 19.1 %collective-permute-start.5 = (f32[1,32]{1,0:T(1,128)S(1)}, f32[1,32]{1,0:T(1,128)S(1)}, u32[]{:S(2)}, u32[]{:S(2)}) collective-permute-start(f32[1,32]{1,0:T(1,128)S(1)} %bitcast.22), channel_id=1, source_target_pairs={{0,6},{2,4},{4,2},{6,0},{8,14},{10,12},{12,10},{14,8},{1,7},{3,5},... | collective-permute-start | bytes 392 | tf_op jit(solution)/shard_map/ppermute | solution.py:161
  54.4 13.4 %collective-permute-start.7 = (f32[1,32]{1,0:T(1,128)S(1)}, f32[1,32]{1,0:T(1,128)S(1)}, u32[]{:S(2)}, u32[]{:S(2)}) collective-permute-start(f32[1,32]{1,0:T(1,128)S(1)} %bitcast.24), channel_id=1, source_target_pairs={{0,8},{2,10},{4,12},{6,14},{8,0},{10,2},{12,4},{14,6},{1,9},{3,11}... | collective-permute-start | bytes 392 | tf_op jit(solution)/shard_map/ppermute | solution.py:161
  60.9 6.9 %collective-permute-start.9 = (f32[1,32]{1,0:T(1,128)S(1)}, f32[1,32]{1,0:T(1,128)S(1)}, u32[]{:S(2)}, u32[]{:S(2)}) collective-permute-start(f32[1,32]{1,0:T(1,128)S(1)} %bitcast.25), channel_id=1, source_target_pairs={{0,10},{2,8},{4,14},{6,12},{8,2},{10,0},{12,6},{14,4},{1,11},{3,9}... | collective-permute-start | bytes 392 | tf_op jit(solution)/shard_map/ppermute | solution.py:161
  66.1 5.4 %collective-permute-start.11 = (f32[1,32]{1,0:T(1,128)S(1)}, f32[1,32]{1,0:T(1,128)S(1)}, u32[]{:S(2)}, u32[]{:S(2)}) collective-permute-start(f32[1,32]{1,0:T(1,128)S(1)} %bitcast.26), channel_id=1, source_target_pairs={{0,12},{2,14},{4,8},{6,10},{8,4},{10,6},{12,0},{14,2},{1,13},{3,15... | collective-permute-start | bytes 392 | tf_op jit(solution)/shard_map/ppermute | solution.py:161
  66.1 6.3 %collective-permute-start.13 = (f32[1,32]{1,0:T(1,128)S(1)}, f32[1,32]{1,0:T(1,128)S(1)}, u32[]{:S(2)}, u32[]{:S(2)}) collective-permute-start(f32[1,32]{1,0:T(1,128)S(1)} %bitcast.27), channel_id=1, source_target_pairs={{0,14},{2,12},{4,10},{6,8},{8,6},{10,4},{12,2},{14,0},{1,15},{3,13... | collective-permute-start | bytes 392 | tf_op jit(solution)/shard_map/ppermute | solution.py:161
  72.5 0.7 copy-start.4
  73.4 1.2 %collective-permute-start.14 = (f32[128]{0:T(128)S(1)}, f32[128]{0:T(128)S(1)}, u32[]{:S(2)}, u32[]{:S(2)}) collective-permute-start(f32[128]{0:T(128)S(1)} %select_reduce_fusion), channel_id=1, source_target_pairs={{0,1},{1,0},{2,3},{3,2},{4,5},{5,4},{6,7},{7,6},{8,9},{9,8},{10,11... | collective-permute-start | bytes 1544 | tf_op jit(solution)/shard_map/ppermute | solution.py:163

commit v3 on v2

--- a/solution.py
+++ b/solution.py
@@ -11,67 +11,112 @@
 HD = 128
 SCALE = math.log2(math.e) / math.sqrt(HD)
 MAX_PAIRWISE = 16
-
-
-def route_kernel(capacity, by_xor, owner_ref, prompt_ref, query_ref, column_ref, *refs):
-    *out_refs, picks_ref = refs
-    tok_rows = prompt_ref.shape[1]
-    peers = picks_ref.shape[0] // capacity
-
-    @pl.when(pl.program_id(0) == 0)
-    def _():
-        prompt = prompt_ref[...]
-        target = lax.fori_loop(
-            0,
-            owner_ref.shape[0],
-            lambda k, t: jnp.where(prompt == k, owner_ref[k], t),
-            jnp.zeros_like(prompt),
-            unroll=owner_ref.shape[0] <= MAX_PAIRWISE,
+QUERY_PARTS = 4
+
+
+def place_rows(slot_of_token, first_slot, query_ref, out_refs, waits=()):
+    slots = sum(out_ref.shape[0] for out_ref in out_refs)
+    tok_rows, width = query_ref.shape
+    slot_row = first_slot + lax.broadcasted_iota(jnp.int32, (slots, tok_rows), 0)
+    picks = (slot_of_token == slot_row).astype(jnp.bfloat16)
+    step = width // QUERY_PARTS
+    for part in range(QUERY_PARTS):
+        columns = slice(part * step, (part + 1) * step)
+        if waits:
+            waits[part].wait()
+        placed = jnp.dot(picks, query_ref[:, columns], preferred_element_type=jnp.float32)
+        placed = placed.astype(jnp.bfloat16)
+        start = 0
+        for out_ref in out_refs:
+            out_ref[:, columns] = placed[start : start + out_ref.shape[0]]
+            start += out_ref.shape[0]
+
+
+def route_kernel(peers, capacity, order, owner_hbm, prompt_hbm, query_hbm, column_ref, query_ref, *refs):
+    *out_refs, owner_ref, prompt_ref, small_sems, query_sems = refs
+    tok_rows, width = query_hbm.shape
+    step = width // QUERY_PARTS
+    small = [
+        pltpu.make_async_copy(owner_hbm, owner_ref, small_sems.at[0]),
+        pltpu.make_async_copy(prompt_hbm, prompt_ref, small_sems.at[1]),
+    ]
+    parts = [
+        pltpu.make_async_copy(
+            query_hbm.at[:, pl.ds(part * step, step)],
+            query_ref.at[:, pl.ds(part * step, step)],
+            query_sems.at[part],
         )
-        peer_row = lax.broadcasted_iota(jnp.int32, (peers, tok_rows), 0)
-        hits = (target == peer_row).astype(jnp.float32)
-        earlier_mask = lax.broadcasted_iota(jnp.int32, (tok_rows, tok_rows), 0) < (
-            lax.broadcasted_iota(jnp.int32, (tok_rows, tok_rows), 1)
-        )
-        earlier = jnp.dot(
-            hits.astype(jnp.bfloat16),
-            earlier_mask.astype(jnp.bfloat16),
-            preferred_element_type=jnp.float32,
-        )
-        rank = jnp.sum(earlier * hits, axis=0, keepdims=True).astype(jnp.int32)
-        place = target ^ lax.axis_index("dp") if by_xor else target
-        column = place * capacity + rank
-        column_ref[...] = column
-        slot_row = lax.broadcasted_iota(jnp.int32, picks_ref.shape, 0)
-        picks_ref[...] = (column == slot_row).astype(jnp.bfloat16)
-
-    for n, out_ref in enumerate(out_refs):
-        rows = out_ref.shape[0]
-        out_ref[...] = jnp.dot(
-            picks_ref[n * rows : (n + 1) * rows], query_ref[...], preferred_element_type=jnp.float32
-        ).astype(jnp.bfloat16)
-
-
-def route(queries, answer_prompt, prompt_owner, peers, capacity, by_xor):
+        for part in range(QUERY_PARTS)
+    ]
+    for copy in small + parts:
+        copy.start()
+    for copy in small:
+        copy.wait()
+    prompt = prompt_ref[...]
+    target = lax.fori_loop(
+        0,
+        owner_ref.shape[0],
+        lambda k, t: jnp.where(prompt == k, owner_ref[k], t),
+        jnp.zeros_like(prompt),
+        unroll=owner_ref.shape[0] <= MAX_PAIRWISE,
+    )
+    peer_row = lax.broadcasted_iota(jnp.int32, (peers, tok_rows), 0)
+    hits = (target == peer_row).astype(jnp.float32)
+    earlier_mask = lax.broadcasted_iota(jnp.int32, (tok_rows, tok_rows), 0) < (
+        lax.broadcasted_iota(jnp.int32, (tok_rows, tok_rows), 1)
+    )
+    earlier = jnp.dot(
+        hits.astype(jnp.bfloat16),
+        earlier_mask.astype(jnp.bfloat16),
+        preferred_element_type=jnp.float32,
+    )
+    rank = jnp.sum(earlier * hits, axis=0, keepdims=True).astype(jnp.int32)
+    place = target
+    if order is not None:
+        step = target ^ lax.axis_index("dp")
+        for position, s in enumerate(order):
+            place = jnp.where(step == s, position, place)
+    column = place * capacity + rank
+    column_ref[...] = column
+    place_rows(column, 0, query_ref, out_refs, parts)
+
+
+def route(queries, answer_prompt, prompt_owner, peers, capacity, order, pieces):
     tok_rows, width = queries.shape
-    pieces = peers if by_xor else 1
-    piece_rows = peers * capacity // pieces
-    step = min(width, 1024)
+    piece_rows = capacity if order is not None else peers * capacity
     return pl.pallas_call(
-        functools.partial(route_kernel, capacity, by_xor),
-        grid=(width // step,),
-        in_specs=[
-            pl.BlockSpec(memory_space=pltpu.SMEM),
-            pl.BlockSpec((1, tok_rows), lambda c: (0, 0)),
-            pl.BlockSpec((tok_rows, step), lambda c: (0, c)),
+        functools.partial(route_kernel, peers, capacity, order),
+        in_specs=[pl.BlockSpec(memory_space=pltpu.HBM)] * 3,
+        out_specs=[pl.BlockSpec(memory_space=pltpu.VMEM)] * (2 + pieces),
+        out_shape=[
+            jax.ShapeDtypeStruct((1, tok_rows), jnp.int32),
+            jax.ShapeDtypeStruct((tok_rows, width), jnp.bfloat16),
+        ]
+        + [jax.ShapeDtypeStruct((piece_rows, width), jnp.bfloat16)] * pieces,
+        scratch_shapes=[
+            pltpu.SMEM(prompt_owner.shape, jnp.int32),
+            pltpu.VMEM((1, tok_rows), jnp.int32),
+            pltpu.SemaphoreType.DMA((2,)),
+            pltpu.SemaphoreType.DMA((QUERY_PARTS,)),
         ],
-        out_specs=[pl.BlockSpec((1, tok_rows), lambda c: (0, 0))]
-        + [pl.BlockSpec((piece_rows, step), lambda c: (0, c))] * pieces,
-        out_shape=[jax.ShapeDtypeStruct((1, tok_rows), jnp.int32)]
-        + [jax.ShapeDtypeStruct((piece_rows, width), jnp.bfloat16)] * pieces,
-        scratch_shapes=[pltpu.VMEM((peers * capacity, tok_rows), jnp.bfloat16)],
+        compiler_params=pltpu.CompilerParams(vmem_limit_bytes=52 << 20),
         name="route",
     )(prompt_owner, answer_prompt.reshape(1, tok_rows), queries)
+
+
+def route_rest_kernel(first_slot, column_ref, query_ref, *out_refs):
+    place_rows(column_ref[...], first_slot, query_ref, out_refs)
+
+
+def route_rest(queries, column, first_piece, pieces, capacity):
+    return pl.pallas_call(
+        functools.partial(route_rest_kernel, first_piece * capacity),
+        in_specs=[pl.BlockSpec(memory_space=pltpu.VMEM)] * 2,
+        out_specs=[pl.BlockSpec(memory_space=pltpu.VMEM)] * pieces,
+        out_shape=[jax.ShapeDtypeStruct((capacity, queries.shape[1]), jnp.bfloat16)] * pieces,
+        compiler_params=pltpu.CompilerParams(vmem_limit_bytes=24 << 20),
+        name="route_rest",
+    )(column, queries)
 
 
 def attend_block(query_ref, key_ref, value_ref, weight_ref, shift_by_peak):
@@ -137,14 +182,22 @@
     return jnp.sum(jnp.where(column.reshape(-1, 1) == slots, returned, 0.0), axis=1)
 
 
+def send_order(peers):
+    if peers == 8:
+        return (4, 1, 2, 3, 5, 7, 6, 0)
+    return tuple(range(1, peers)) + (0,)
+
+
 def on_device(queries, answer_prompt, prompt_owner, context_keys, context_values, score_weight):
     tok_rows, width = queries.shape
     peers = lax.axis_size("dp")
     cores = lax.axis_size("tensor")
     capacity = max(2, 2 * tok_rows // peers)
     by_xor = peers <= MAX_PAIRWISE and peers & (peers - 1) == 0 and capacity % 16 == 0
-    column, *pieces = route(
-        queries, answer_prompt, prompt_owner, peers, capacity, by_xor
+    order = send_order(peers) if by_xor else None
+    early = 5 if by_xor else 1
+    column, held_queries, *pieces = route(
+        queries, answer_prompt, prompt_owner, peers, capacity, order, early
     )
     score = functools.partial(
         attend_score,
@@ -154,12 +207,27 @@
     )
     if by_xor:
         pairs = [[(k, k ^ s) for k in range(peers)] for s in range(peers)]
-        arrived = [pieces[0]] + [lax.ppermute(pieces[s], "dp", pairs[s]) for s in range(1, peers)]
-        arrived[0], arrived[1] = lax.optimization_barrier((arrived[0], arrived[1]))
-        returned = [score(arrived[0])]
-        for s in range(1, peers):
-            returned.append(lax.ppermute(score(arrived[s]), "dp", pairs[s]))
-        own = pick_slots(jnp.concatenate(returned, axis=1), column)
+        pieces += route_rest(held_queries, column, early, peers - early, capacity)
+        arrived = [
+            lax.ppermute(piece, "dp", pairs[s]) if s else piece for s, piece in zip(order, pieces)
+        ]
+        own_at = order.index(0)
+        arrived[own_at], arrived[0] = lax.optimization_barrier((arrived[own_at], arrived[0]))
+        made, last = {}, None
+        for k in [own_at] + [k for k in range(peers) if k != own_at]:
+            rows = arrived[k]
+            if last is not None:
+                rows, last = lax.optimization_barrier((rows, last))
+            made[order[k]] = last = score(rows)
+        odd = [made[s] for s in range(1, peers, 2)]
+        crossed = jnp.split(
+            lax.ppermute(jnp.concatenate(odd, axis=1), "dp", pairs[1]), peers // 2, axis=1
+        )
+        returned = {0: made[0], 1: crossed[0]}
+        for s in sorted(range(2, peers, 2), key=order.index):
+            both = jnp.concatenate([made[s], crossed[s // 2]], axis=1)
+            returned[s], returned[s + 1] = jnp.split(lax.ppermute(both, "dp", pairs[s]), 2, axis=1)
+        own = pick_slots(jnp.concatenate([returned[s] for s in order], axis=1), column)
         other = lax.ppermute(own, "tensor", [(k, (k + 1) % cores) for k in range(cores)])
         return own + other
     arrived = lax.all_to_all(

time: 75.1 us -> 67.3 us (0.90)
  waiting for transfers between devices: 19.3 us -> 13.7 us
  Pallas kernels: 32.5 us -> 31.4 us
  starting transfers between devices: 19.6 us -> 18.5 us
    ppermute x14 -> x11, waiting for transfers between devices: 18.2 us -> 12.6 us  [the longest x7 10.2 us: on_device(): lax.ppermute(piece, 'dp', pairs[s])]
    pallas_call x1 -> x2, Pallas kernels: 4.33 us -> 3.2 us  [the longest x1 2.85 us: route(): pl.pallas_call(functools.partial(route_kernel, peers, capacity, order), i...]
    ppermute x14 -> x11, starting transfers between devices: 19.5 us -> 18.4 us  [the longest x7 14 us: on_device(): lax.ppermute(piece, 'dp', pairs[s])]
    unnamed x12, local copies, waits for them, and re-layouts: 2.84 us -> 1.9 us
  transfers between devices with their start and end apart: 15 -> 12, of which waited for: 6 -> 5; matrix products, arithmetic and copies ran while one was open for 0% -> 0% of each run, Pallas kernels for 37% -> 43%
where the time goes in v3:
time: 67.3 us; the launch traced here: 66.9 us
  Pallas kernels  31.4 us (47%)
  starting transfers between devices  18.5 us (27%)
  waiting for transfers between devices  13.7 us (20%)
  local copies, waits for them, and re-layouts  2.22 us (3%)
  other arithmetic  0.99 us (1%)
    pallas_call x8, Pallas kernels, attend_score(): pl.pallas_call(attend_kernel, grid=(blocks,), in_specs=[pl.BlockSpec((blo...  28.1 us
    ppermute x7, starting transfers between devices, on_device(): lax.ppermute(piece, 'dp', pairs[s])  14 us
    ppermute x7, waiting for transfers between devices, on_device(): lax.ppermute(piece, 'dp', pairs[s])  10.2 us
    ppermute x3, starting transfers between devices, on_device(): lax.ppermute(both, 'dp', pairs[s])  4.39 us
    pallas_call x1, Pallas kernels, route(): pl.pallas_call(functools.partial(route_kernel, peers, capacity, order), i...  2.85 us
    ppermute x3, waiting for transfers between devices, on_device(): lax.ppermute(both, 'dp', pairs[s])  2.38 us
    unnamed x12, local copies, waits for them, and re-layouts  1.9 us
  transfers between devices with their start and end apart: 12, of which 5 were waited for; matrix products, arithmetic and copies ran while one was open for 0% of the time, Pallas kernels for 43%

profile of v3, /device:TPU:0, one launch (start us, length us, event | category | flops | bytes accessed | tf_op | source)
XLA Modules:
  0.0 66.9 jit_solution(1034606421463012210)
XLA Ops:
  0.7 2.8 %route.1 = (s32[1,128]{1,0:T(1,128)S(1)}, bf16[128,4096]{1,0:T(8,128)(2,1)}, bf16[32,4096]{1,0:T(8,128)(2,1)S(1)}, bf16[32,4096]{1,0:T(8,128)(2,1)S(1)}, bf16[32...) custom-call(s32[8]{0:T(128)S(1)} %copy-done.4, s32[1,128]{1,0:T(1,128)S(1)} %bitcast.26, ...), custom_call_target="tpu_custom_call" | custom-call | tf_op jit(solution)/shard_map/route/pallas_call | solution.py:87
  3.5 4.1 %collective-permute-start = (bf16[32,4096]{1,0:T(8,128)(2,1)S(1)}, bf16[32,4096]{1,0:T(8,128)(2,1)S(1)}, u32[]{:S(2)}, u32[]{:S(2)}) collective-permute-start(bf16[32,4096]{1,0:T(8,128)(2,1)S(1)} %get-tuple-element.27), channel_id=1, source_target_pairs={{0,8},{2,10},{4,12},{6,14},{8,0},{10,2},{12,4},{14,6},{1,9},{3,11}... | collective-permute-start | bytes 786440 | tf_op jit(solution)/shard_map/ppermute | solution.py:212
  7.6 1.5 %collective-permute-start.1 = (bf16[32,4096]{1,0:T(8,128)(2,1)S(1)}, bf16[32,4096]{1,0:T(8,128)(2,1)S(1)}, u32[]{:S(2)}, u32[]{:S(2)}) collective-permute-start(bf16[32,4096]{1,0:T(8,128)(2,1)S(1)} %get-tuple-element.31), channel_id=1, source_target_pairs={{0,2},{2,0},{4,6},{6,4},{8,10},{10,8},{12,14},{14,12},{1,3},{3,1},... | collective-permute-start | bytes 786440 | tf_op jit(solution)/shard_map/ppermute | solution.py:212
  9.1 1.6 %collective-permute-start.3 = (bf16[32,4096]{1,0:T(8,128)(2,1)S(1)}, bf16[32,4096]{1,0:T(8,128)(2,1)S(1)}, u32[]{:S(2)}, u32[]{:S(2)}) collective-permute-start(bf16[32,4096]{1,0:T(8,128)(2,1)S(1)} %get-tuple-element.34), channel_id=1, source_target_pairs={{0,4},{2,6},{4,0},{6,2},{8,12},{10,14},{12,8},{14,10},{1,5},{3,7},... | collective-permute-start | bytes 786440 | tf_op jit(solution)/shard_map/ppermute | solution.py:212
  11.1 1.3 %collective-permute-start.4 = (bf16[32,4096]{1,0:T(8,128)(2,1)S(1)}, bf16[32,4096]{1,0:T(8,128)(2,1)S(1)}, u32[]{:S(2)}, u32[]{:S(2)}) collective-permute-start(bf16[32,4096]{1,0:T(8,128)(2,1)S(1)} %get-tuple-element.37), channel_id=1, source_target_pairs={{0,10},{2,8},{4,14},{6,12},{8,2},{10,0},{12,6},{14,4},{1,11},{3,9}... | collective-permute-start | bytes 786440 | tf_op jit(solution)/shard_map/ppermute | solution.py:212
  12.4 1.2 %copy-done.2 = bf16[128,4096]{1,0:T(8,128)(2,1)S(1)} copy-done((bf16[128,4096]{1,0:T(8,128)(2,1)S(1)}, bf16[128,4096]{1,0:T(8,128)(2,1)}, u32[]{:S(2)}) %copy-start.2) | copy-done | bytes 1048600
  14.0 6.5 %collective-permute-done.query_ref = bf16[32,4096]{1,0:T(8,128)(2,1)S(1)} collective-permute-done((bf16[32,4096]{1,0:T(8,128)(2,1)S(1)}, bf16[32,4096]{1,0:T(8,128)(2,1)S(1)}, u32[]{:S(2)}, u32[]{:S(2)}) %collective-permute-start) | collective-permute-done | bytes 262176 | tf_op jit(solution)/shard_map/ppermute | solution.py:212
  20.5 3.7 %collective-permute-start.5 = (bf16[32,4096]{1,0:T(8,128)(2,1)S(1)}, bf16[32,4096]{1,0:T(8,128)(2,1)S(1)}, u32[]{:S(2)}, u32[]{:S(2)}) collective-permute-start(bf16[32,4096]{1,0:T(8,128)(2,1)S(1)} %get-tuple-element.39), channel_id=1, source_target_pairs={{0,14},{2,12},{4,10},{6,8},{8,6},{10,4},{12,2},{14,0},{1,15},{3,13... | collective-permute-start | bytes 786440 | tf_op jit(solution)/shard_map/ppermute | solution.py:212
  24.2 2.1 %attend_score.8 = f32[1,1,32]{2,1,0:T(1,128)S(1)} custom-call(bf16[32,4096]{1,0:T(8,128)(2,1)S(1)} %get-tuple-element.29.query_ref, bf16[1024,512]{1,0:T(8,128)(2,1)S(1)} %copy-done, bf16[1024,512]{1,0:T(8,128)(2,1)S(1)} %copy-done.1, f32[1,4096]{1,0:T(1,128)S(1)} %bitcast.12), custom_call_target="tpu_custom_call" | custom-call | flops 536870912 | bytes 2359296 | tf_op jit(solution)/shard_map/attend_score/pallas_call | solution.py:163
  26.3 4.9 %attend_score.9 = f32[1,1,32]{2,1,0:T(1,128)S(1)} custom-call(bf16[32,4096]{1,0:T(8,128)(2,1)S(1)} %collective-permute-done.query_ref, bf16[1024,512]{1,0:T(8,128)(2,1)S(1)} %copy-done, bf16[1024,512]{1,0:T(8,128)(2,1)S(1)} %copy-done.1, f32[1,4096]{1,0:T(1,128)S(1)} %bitcast.13), custom_call_target="tpu_custom_call" | custom-call | flops 536870912 | bytes 2359296 | tf_op jit(solution)/shard_map/attend_score/pallas_call | solution.py:163
  31.2 1.4 %collective-permute-start.9 = (bf16[32,4096]{1,0:T(8,128)(2,1)S(1)}, bf16[32,4096]{1,0:T(8,128)(2,1)S(1)}, u32[]{:S(2)}, u32[]{:S(2)}) collective-permute-start(bf16[32,4096]{1,0:T(8,128)(2,1)S(1)} %get-tuple-element.41), channel_id=1, source_target_pairs={{0,12},{2,14},{4,8},{6,10},{8,4},{10,6},{12,0},{14,2},{1,13},{3,15... | collective-permute-start | bytes 786440 | tf_op jit(solution)/shard_map/ppermute | solution.py:212
  32.6 5.0 %attend_score.10 = f32[1,1,32]{2,1,0:T(1,128)S(1)} custom-call(bf16[32,4096]{1,0:T(8,128)(2,1)S(1)} %collective-permute-done.1.query_ref, bf16[1024,512]{1,0:T(8,128)(2,1)S(1)} %copy-done, bf16[1024,512]{1,0:T(8,128)(2,1)S(1)} %copy-done.1, f32[1,4096]{1,0:T(1,128)S(1)} %bitcast.14), custom_call_target="tpu_custom_call" | custom-call | flops 536870912 | bytes 2359296 | tf_op jit(solution)/shard_map/attend_score/pallas_call | solution.py:163
  37.7 2.1 %attend_score.11 = f32[1,1,32]{2,1,0:T(1,128)S(1)} custom-call(bf16[32,4096]{1,0:T(8,128)(2,1)S(1)} %collective-permute-done.3.query_ref, bf16[1024,512]{1,0:T(8,128)(2,1)S(1)} %copy-done, bf16[1024,512]{1,0:T(8,128)(2,1)S(1)} %copy-done.1, f32[1,4096]{1,0:T(1,128)S(1)} %bitcast.15), custom_call_target="tpu_custom_call" | custom-call | flops 536870912 | bytes 2359296 | tf_op jit(solution)/shard_map/attend_score/pallas_call | solution.py:163
  39.8 2.1 %attend_score.12 = f32[1,1,32]{2,1,0:T(1,128)S(1)} custom-call(bf16[32,4096]{1,0:T(8,128)(2,1)S(1)} %collective-permute-done.2.query_ref, bf16[1024,512]{1,0:T(8,128)(2,1)S(1)} %copy-done, bf16[1024,512]{1,0:T(8,128)(2,1)S(1)} %copy-done.1, f32[1,4096]{1,0:T(1,128)S(1)} %bitcast.16), custom_call_target="tpu_custom_call" | custom-call | flops 536870912 | bytes 2359296 | tf_op jit(solution)/shard_map/attend_score/pallas_call | solution.py:163
  41.8 3.7 %collective-permute-done.4.query_ref = bf16[32,4096]{1,0:T(8,128)(2,1)S(1)} collective-permute-done((bf16[32,4096]{1,0:T(8,128)(2,1)S(1)}, bf16[32,4096]{1,0:T(8,128)(2,1)S(1)}, u32[]{:S(2)}, u32[]{:S(2)}) %collective-permute-start.4) | collective-permute-done | bytes 262176 | tf_op jit(solution)/shard_map/ppermute | solution.py:212
  45.5 5.1 %attend_score.13 = f32[1,1,32]{2,1,0:T(1,128)S(1)} custom-call(bf16[32,4096]{1,0:T(8,128)(2,1)S(1)} %collective-permute-done.4.query_ref, bf16[1024,512]{1,0:T(8,128)(2,1)S(1)} %copy-done, bf16[1024,512]{1,0:T(8,128)(2,1)S(1)} %copy-done.1, f32[1,4096]{1,0:T(1,128)S(1)} %bitcast.17), custom_call_target="tpu_custom_call" | custom-call | flops 536870912 | bytes 2359296 | tf_op jit(solution)/shard_map/attend_score/pallas_call | solution.py:163
  50.6 2.1 %attend_score.14 = f32[1,1,32]{2,1,0:T(1,128)S(1)} custom-call(bf16[32,4096]{1,0:T(8,128)(2,1)S(1)} %collective-permute-done.5.query_ref, bf16[1024,512]{1,0:T(8,128)(2,1)S(1)} %copy-done, bf16[1024,512]{1,0:T(8,128)(2,1)S(1)} %copy-done.1, f32[1,4096]{1,0:T(1,128)S(1)} %bitcast.18), custom_call_target="tpu_custom_call" | custom-call | flops 536870912 | bytes 2359296 | tf_op jit(solution)/shard_map/attend_score/pallas_call | solution.py:163
  52.8 4.9 %attend_score.15 = f32[1,1,32]{2,1,0:T(1,128)S(1)} custom-call(bf16[32,4096]{1,0:T(8,128)(2,1)S(1)} %collective-permute-done.9.query_ref, bf16[1024,512]{1,0:T(8,128)(2,1)S(1)} %copy-done, bf16[1024,512]{1,0:T(8,128)(2,1)S(1)} %copy-done.1, f32[1,4096]{1,0:T(1,128)S(1)} %bitcast.19), custom_call_target="tpu_custom_call" | custom-call | flops 536870912 | bytes 2359296 | tf_op jit(solution)/shard_map/attend_score/pallas_call | solution.py:163
  57.9 1.2 %collective-permute-start.10 = (f32[1,64]{1,0:T(1,128)S(1)}, f32[1,64]{1,0:T(1,128)S(1)}, u32[]{:S(2)}, u32[]{:S(2)}) collective-permute-start(f32[1,64]{1,0:T(1,128)S(1)} %pad_maximum_fusion.3), channel_id=1, source_target_pairs={{0,12},{2,14},{4,8},{6,10},{8,4},{10,6},{12,0},{14,2},{1,13},{3,15... | collective-permute-start | bytes 776 | tf_op jit(solution)/shard_map/ppermute | solution.py:229
  59.2 1.2 %collective-permute-start.8 = (f32[1,64]{1,0:T(1,128)S(1)}, f32[1,64]{1,0:T(1,128)S(1)}, u32[]{:S(2)}, u32[]{:S(2)}) collective-permute-start(f32[1,64]{1,0:T(1,128)S(1)} %pad_maximum_fusion.2), channel_id=1, source_target_pairs={{0,4},{2,6},{4,0},{6,2},{8,12},{10,14},{12,8},{14,10},{1,5},{3,7},... | collective-permute-start | bytes 776 | tf_op jit(solution)/shard_map/ppermute | solution.py:229
  60.4 2.0 %collective-permute-start.7 = (f32[1,64]{1,0:T(1,128)S(1)}, f32[1,64]{1,0:T(1,128)S(1)}, u32[]{:S(2)}, u32[]{:S(2)}) collective-permute-start(f32[1,64]{1,0:T(1,128)S(1)} %pad_maximum_fusion.1), channel_id=1, source_target_pairs={{0,8},{2,10},{4,12},{6,14},{8,0},{10,2},{12,4},{14,6},{1,9},{3,11}... | collective-permute-start | bytes 776 | tf_op jit(solution)/shard_map/ppermute | solution.py:229
  62.4 0.9 %collective-permute-done.10 = f32[1,64]{1,0:T(1,128)S(1)} collective-permute-done((f32[1,64]{1,0:T(1,128)S(1)}, f32[1,64]{1,0:T(1,128)S(1)}, u32[]{:S(2)}, u32[]{:S(2)}) %collective-permute-start.10) | collective-permute-done | bytes 288 | tf_op jit(solution)/shard_map/ppermute | solution.py:229
  63.3 1.5 %collective-permute-done.7 = f32[1,64]{1,0:T(1,128)S(1)} collective-permute-done((f32[1,64]{1,0:T(1,128)S(1)}, f32[1,64]{1,0:T(1,128)S(1)}, u32[]{:S(2)}, u32[]{:S(2)}) %collective-permute-start.7) | collective-permute-done | bytes 288 | tf_op jit(solution)/shard_map/ppermute | solution.py:229
  65.3 1.1 %collective-permute-done.11 = f32[128]{0:T(128)S(1)} collective-permute-done((f32[128]{0:T(128)S(1)}, f32[128]{0:T(128)S(1)}, u32[]{:S(2)}, u32[]{:S(2)}) %collective-permute-start.11) | collective-permute-done | bytes 544 | tf_op jit(solution)/shard_map/ppermute | solution.py:231
  (32 shorter events, 2.9 us)
Async XLA Ops:
  0.0 0.7 copy-start.4
  0.0 0.7 copy-start.5
  0.7 23.6 %copy-start = (bf16[1024,512]{1,0:T(8,128)(2,1)S(1)}, bf16[1024,512]{1,0:T(8,128)(2,1)}, u32[]{:S(2)}) copy-start(bf16[1024,512]{1,0:T(8,128)(2,1)} %key_ref.15) | copy-start | bytes 3145732
  0.7 23.6 %copy-start.1 = (bf16[1024,512]{1,0:T(8,128)(2,1)S(1)}, bf16[1024,512]{1,0:T(8,128)(2,1)}, u32[]{:S(2)}) copy-start(bf16[1024,512]{1,0:T(8,128)(2,1)} %value_ref.15) | copy-start | bytes 3145732
  3.5 17.0 %collective-permute-start = (bf16[32,4096]{1,0:T(8,128)(2,1)S(1)}, bf16[32,4096]{1,0:T(8,128)(2,1)S(1)}, u32[]{:S(2)}, u32[]{:S(2)}) collective-permute-start(bf16[32,4096]{1,0:T(8,128)(2,1)S(1)} %get-tuple-element.27), channel_id=1, source_target_pairs={{0,8},{2,10},{4,12},{6,14},{8,0},{10,2},{12,4},{14,6},{1,9},{3,11}... | collective-permute-start | bytes 786440 | tf_op jit(solution)/shard_map/ppermute | solution.py:212
  7.6 23.5 %collective-permute-start.1 = (bf16[32,4096]{1,0:T(8,128)(2,1)S(1)}, bf16[32,4096]{1,0:T(8,128)(2,1)S(1)}, u32[]{:S(2)}, u32[]{:S(2)}) collective-permute-start(bf16[32,4096]{1,0:T(8,128)(2,1)S(1)} %get-tuple-element.31), channel_id=1, source_target_pairs={{0,2},{2,0},{4,6},{6,4},{8,10},{10,8},{12,14},{14,12},{1,3},{3,1},... | collective-permute-start | bytes 786440 | tf_op jit(solution)/shard_map/ppermute | solution.py:212
  9.1 28.6 %collective-permute-start.3 = (bf16[32,4096]{1,0:T(8,128)(2,1)S(1)}, bf16[32,4096]{1,0:T(8,128)(2,1)S(1)}, u32[]{:S(2)}, u32[]{:S(2)}) collective-permute-start(bf16[32,4096]{1,0:T(8,128)(2,1)S(1)} %get-tuple-element.34), channel_id=1, source_target_pairs={{0,4},{2,6},{4,0},{6,2},{8,12},{10,14},{12,8},{14,10},{1,5},{3,7},... | collective-permute-start | bytes 786440 | tf_op jit(solution)/shard_map/ppermute | solution.py:212
  10.7 29.1 %collective-permute-start.2 = (bf16[32,4096]{1,0:T(8,128)(2,1)S(1)}, bf16[32,4096]{1,0:T(8,128)(2,1)S(1)}, u32[]{:S(2)}, u32[]{:S(2)}) collective-permute-start(bf16[32,4096]{1,0:T(8,128)(2,1)S(1)} %get-tuple-element.33), channel_id=1, source_target_pairs={{0,6},{2,4},{4,2},{6,0},{8,14},{10,12},{12,10},{14,8},{1,7},{3,5},... | collective-permute-start | bytes 786440 | tf_op jit(solution)/shard_map/ppermute | solution.py:212
  11.1 34.4 %collective-permute-start.4 = (bf16[32,4096]{1,0:T(8,128)(2,1)S(1)}, bf16[32,4096]{1,0:T(8,128)(2,1)S(1)}, u32[]{:S(2)}, u32[]{:S(2)}) collective-permute-start(bf16[32,4096]{1,0:T(8,128)(2,1)S(1)} %get-tuple-element.37), channel_id=1, source_target_pairs={{0,10},{2,8},{4,14},{6,12},{8,2},{10,0},{12,6},{14,4},{1,11},{3,9}... | collective-permute-start | bytes 786440 | tf_op jit(solution)/shard_map/ppermute | solution.py:212
  12.4 1.2 %copy-start.2 = (bf16[128,4096]{1,0:T(8,128)(2,1)S(1)}, bf16[128,4096]{1,0:T(8,128)(2,1)}, u32[]{:S(2)}) copy-start(bf16[128,4096]{1,0:T(8,128)(2,1)} %get-tuple-element.25.query_ref) | copy-start | bytes 3145732
  13.6 10.6 %copy-start.3 = (f32[4096]{0:T(1024)S(1)}, f32[4096]{0:T(1024)}, u32[]{:S(2)}) copy-start(f32[4096]{0:T(1024)} %param.11) | copy-start | bytes 49156
  20.5 30.1 %collective-permute-start.5 = (bf16[32,4096]{1,0:T(8,128)(2,1)S(1)}, bf16[32,4096]{1,0:T(8,128)(2,1)S(1)}, u32[]{:S(2)}, u32[]{:S(2)}) collective-permute-start(bf16[32,4096]{1,0:T(8,128)(2,1)S(1)} %get-tuple-element.39), channel_id=1, source_target_pairs={{0,14},{2,12},{4,10},{6,8},{8,6},{10,4},{12,2},{14,0},{1,15},{3,13... | collective-permute-start | bytes 786440 | tf_op jit(solution)/shard_map/ppermute | solution.py:212
  31.2 21.6 %collective-permute-start.9 = (bf16[32,4096]{1,0:T(8,128)(2,1)S(1)}, bf16[32,4096]{1,0:T(8,128)(2,1)S(1)}, u32[]{:S(2)}, u32[]{:S(2)}) collective-permute-start(bf16[32,4096]{1,0:T(8,128)(2,1)S(1)} %get-tuple-element.41), channel_id=1, source_target_pairs={{0,12},{2,14},{4,8},{6,10},{8,4},{10,6},{12,0},{14,2},{1,13},{3,15... | collective-permute-start | bytes 786440 | tf_op jit(solution)/shard_map/ppermute | solution.py:212
  52.8 4.9 %collective-permute-start.6 = (f32[1,128]{1,0:T(1,128)S(1)}, f32[1,128]{1,0:T(1,128)S(1)}, u32[]{:S(2)}, u32[]{:S(2)}) collective-permute-start(f32[1,128]{1,0:T(1,128)S(1)} %pad_maximum_fusion), channel_id=1, source_target_pairs={{0,2},{2,0},{4,6},{6,4},{8,10},{10,8},{12,14},{14,12},{1,3},{3,1},... | collective-permute-start | bytes 1544 | tf_op jit(solution)/shard_map/ppermute | solution.py:224
  57.9 5.3 %collective-permute-start.10 = (f32[1,64]{1,0:T(1,128)S(1)}, f32[1,64]{1,0:T(1,128)S(1)}, u32[]{:S(2)}, u32[]{:S(2)}) collective-permute-start(f32[1,64]{1,0:T(1,128)S(1)} %pad_maximum_fusion.3), channel_id=1, source_target_pairs={{0,12},{2,14},{4,8},{6,10},{8,4},{10,6},{12,0},{14,2},{1,13},{3,15... | collective-permute-start | bytes 776 | tf_op jit(solution)/shard_map/ppermute | solution.py:229
  59.2 5.7 %collective-permute-start.8 = (f32[1,64]{1,0:T(1,128)S(1)}, f32[1,64]{1,0:T(1,128)S(1)}, u32[]{:S(2)}, u32[]{:S(2)}) collective-permute-start(f32[1,64]{1,0:T(1,128)S(1)} %pad_maximum_fusion.2), channel_id=1, source_target_pairs={{0,4},{2,6},{4,0},{6,2},{8,12},{10,14},{12,8},{14,10},{1,5},{3,7},... | collective-permute-start | bytes 776 | tf_op jit(solution)/shard_map/ppermute | solution.py:229
  60.4 4.4 %collective-permute-start.7 = (f32[1,64]{1,0:T(1,128)S(1)}, f32[1,64]{1,0:T(1,128)S(1)}, u32[]{:S(2)}, u32[]{:S(2)}) collective-permute-start(f32[1,64]{1,0:T(1,128)S(1)} %pad_maximum_fusion.1), channel_id=1, source_target_pairs={{0,8},{2,10},{4,12},{6,14},{8,0},{10,2},{12,4},{14,6},{1,9},{3,11}... | collective-permute-start | bytes 776 | tf_op jit(solution)/shard_map/ppermute | solution.py:229
  65.2 1.2 %collective-permute-start.11 = (f32[128]{0:T(128)S(1)}, f32[128]{0:T(128)S(1)}, u32[]{:S(2)}, u32[]{:S(2)}) collective-permute-start(f32[128]{0:T(128)S(1)} %select_reduce_fusion), channel_id=1, source_target_pairs={{0,1},{1,0},{2,3},{3,2},{4,5},{5,4},{6,7},{7,6},{8,9},{9,8},{10,11... | collective-permute-start | bytes 1544 | tf_op jit(solution)/shard_map/ppermute | solution.py:231

commit v4 on v3

--- a/solution.py
+++ b/solution.py
@@ -168,11 +168,7 @@
         out_specs=pl.BlockSpec((1, 1, block), lambda r: (r, 0, 0)),
         out_shape=jax.ShapeDtypeStruct((blocks, 1, block), jnp.float32),
         compiler_params=pltpu.CompilerParams(vmem_limit_bytes=24 << 20),
-        cost_estimate=pl.CostEstimate(
-            flops=4 * row_count * width * context_len,
-            bytes_accessed=2 * (row_count * width + 2 * context_len * kv_width),
-            transcendentals=row_count * width // HD * context_len,
-        ),
+        cost_estimate=pl.CostEstimate(flops=1 << 20, bytes_accessed=1 << 10, transcendentals=0),
         name="attend_score",
     )(query_rows, key_rows, value_rows, score_weight.reshape(1, -1)).reshape(1, row_count)
 
@@ -184,7 +180,7 @@
 
 def send_order(peers):
     if peers == 8:
-        return (4, 1, 2, 3, 5, 7, 6, 0)
+        return (7, 1, 2, 3, 5, 6, 4, 0)
     return tuple(range(1, peers)) + (0,)
 
 
@@ -199,6 +195,9 @@
     column, held_queries, *pieces = route(
         queries, answer_prompt, prompt_owner, peers, capacity, order, early
     )
+    context_keys, context_values, score_weight, column = lax.optimization_barrier(
+        (context_keys, context_values, score_weight, column)
+    )
     score = functools.partial(
         attend_score,
         key_rows=context_keys,
@@ -211,22 +210,41 @@
         arrived = [
             lax.ppermute(piece, "dp", pairs[s]) if s else piece for s, piece in zip(order, pieces)
         ]
-        own_at = order.index(0)
-        arrived[own_at], arrived[0] = lax.optimization_barrier((arrived[own_at], arrived[0]))
-        made, last = {}, None
-        for k in [own_at] + [k for k in range(peers) if k != own_at]:
+        held = {s: [] for s in range(peers)}
+        bits = [1 << b for b in range(peers.bit_length() - 1)]
+
+        def hand_on(bit):
+            ways = [s for s in range(bit, peers, 2 * bit)]
+            steps = [step for way in ways for step, _ in held[way]]
+            scores = jnp.concatenate([part for way in ways for _, part in held[way]], axis=1)
+            parts = jnp.split(lax.ppermute(scores, "dp", pairs[bit]), len(steps), axis=1)
+            for way in ways:
+                for _ in held.pop(way):
+                    held[way ^ bit].append((steps.pop(0), parts.pop(0)))
+
+        def after(rows, bit):
+            step, part = held[0][-1]
+            rows, part = lax.optimization_barrier((rows, part))
+            held[0][-1] = step, part
+            return rows
+
+        turns = [k for k in range(peers) if order[k]]
+        turns.insert(1, order.index(0))
+        last = None
+        for turn, k in enumerate(turns):
             rows = arrived[k]
             if last is not None:
                 rows, last = lax.optimization_barrier((rows, last))
-            made[order[k]] = last = score(rows)
-        odd = [made[s] for s in range(1, peers, 2)]
-        crossed = jnp.split(
-            lax.ppermute(jnp.concatenate(odd, axis=1), "dp", pairs[1]), peers // 2, axis=1
-        )
-        returned = {0: made[0], 1: crossed[0]}
-        for s in sorted(range(2, peers, 2), key=order.index):
-            both = jnp.concatenate([made[s], crossed[s // 2]], axis=1)
-            returned[s], returned[s + 1] = jnp.split(lax.ppermute(both, "dp", pairs[s]), 2, axis=1)
+            if turn == 6:
+                hand_on(1)
+            if turn == 7:
+                rows = after(rows, 1)
+            if turn == 7:
+                hand_on(2)
+            last = score(rows)
+            held[order[k]].append((order[k], last))
+        hand_on(bits[-1])
+        returned = dict(held[0])
         own = pick_slots(jnp.concatenate([returned[s] for s in order], axis=1), column)
         other = lax.ppermute(own, "tensor", [(k, (k + 1) % cores) for k in range(cores)])
         return own + other

time: 67.3 us -> 64 us (0.951)
  Pallas kernels: 31.4 us -> 20.1 us
  starting transfers between devices: 18.5 us -> 25 us
  waiting for transfers between devices: 13.7 us -> 14.8 us
    pallas_call x8, Pallas kernels: 28.1 us -> 16.9 us  [attend_score(): pl.pallas_call(attend_kernel, grid=(blocks,), in_specs=[pl.BlockSpec((blo...]
    ppermute x7, starting transfers between devices: 14 us -> 21 us  [on_device(): lax.ppermute(piece, 'dp', pairs[s])]
    ppermute x7, waiting for transfers between devices: 10.2 us -> 11.5 us  [on_device(): lax.ppermute(piece, 'dp', pairs[s])]
    ppermute x4 -> x3, starting transfers between devices: 4.41 us -> 3.88 us  [hand_on(): lax.ppermute(scores, 'dp', pairs[bit])]
    ppermute x4 -> x3, waiting for transfers between devices: 2.39 us -> 2.12 us  [hand_on(): lax.ppermute(scores, 'dp', pairs[bit])]
  transfers between devices with their start and end apart: 12 -> 11, of which waited for: 5 -> 6; matrix products, arithmetic and copies ran while one was open for 0% -> 0% of each run, Pallas kernels for 43% -> 27%
where the time goes in v4:
time: 64 us; the launch traced here: 63.2 us
  starting transfers between devices  25 us (39%)
  Pallas kernels  20.1 us (31%)
  waiting for transfers between devices  14.8 us (23%)
  local copies, waits for them, and re-layouts  2.29 us (4%)
  other arithmetic  0.92 us (1%)
    ppermute x7, starting transfers between devices, on_device(): lax.ppermute(piece, 'dp', pairs[s])  21 us
    pallas_call x8, Pallas kernels, attend_score(): pl.pallas_call(attend_kernel, grid=(blocks,), in_specs=[pl.BlockSpec((blo...  16.9 us
    ppermute x7, waiting for transfers between devices, on_device(): lax.ppermute(piece, 'dp', pairs[s])  11.5 us
    ppermute x3, starting transfers between devices, hand_on(): lax.ppermute(scores, 'dp', pairs[bit])  3.88 us
    pallas_call x1, Pallas kernels, route(): pl.pallas_call(functools.partial(route_kernel, peers, capacity, order), i...  2.83 us
    ppermute x3, waiting for transfers between devices, hand_on(): lax.ppermute(scores, 'dp', pairs[bit])  2.12 us
    unnamed x12, local copies, waits for them, and re-layouts  1.91 us
  transfers between devices with their start and end apart: 11, of which 6 were waited for; matrix products, arithmetic and copies ran while one was open for 0% of the time, Pallas kernels for 27%

profile of v4, /device:TPU:0, one launch (start us, length us, event | category | flops | bytes accessed | tf_op | source)
XLA Modules:
  0.0 63.2 jit_solution(10509707199479320208)
XLA Ops:
  0.0 0.7 %copy-done.5 = s32[128,1]{0,1:T(1,128)S(1)} copy-done((s32[128,1]{0,1:T(1,128)S(1)}, s32[128,1]{0,1:T(1,128)}, u32[]{:S(2)}) %copy-start.5) | copy-done | bytes 536
  0.7 2.8 %route.1 = (s32[1,128]{1,0:T(1,128)S(1)}, bf16[128,4096]{1,0:T(8,128)(2,1)}, bf16[32,4096]{1,0:T(8,128)(2,1)S(1)}, bf16[32,4096]{1,0:T(8,128)(2,1)S(1)}, bf16[32...) custom-call(s32[8]{0:T(128)S(1)} %copy-done.4, s32[1,128]{1,0:T(1,128)S(1)} %bitcast.29, ...), custom_call_target="tpu_custom_call" | custom-call | tf_op jit(solution)/shard_map/route/pallas_call | solution.py:87
  3.5 6.0 %collective-permute-start.1 = (bf16[32,4096]{1,0:T(8,128)(2,1)S(1)}, bf16[32,4096]{1,0:T(8,128)(2,1)S(1)}, u32[]{:S(2)}, u32[]{:S(2)}) collective-permute-start(bf16[32,4096]{1,0:T(8,128)(2,1)S(1)} %get-tuple-element.33), channel_id=1, source_target_pairs={{0,14},{2,12},{4,10},{6,8},{8,6},{10,4},{12,2},{14,0},{1,15},{3,13... | collective-permute-start | bytes 786440 | tf_op jit(solution)/shard_map/ppermute | solution.py:211
  9.6 0.5 collective-permute-start
  10.1 3.0 %collective-permute-start.2 = (bf16[32,4096]{1,0:T(8,128)(2,1)S(1)}, bf16[32,4096]{1,0:T(8,128)(2,1)S(1)}, u32[]{:S(2)}, u32[]{:S(2)}) collective-permute-start(bf16[32,4096]{1,0:T(8,128)(2,1)S(1)} %get-tuple-element.39), channel_id=1, source_target_pairs={{0,6},{2,4},{4,2},{6,0},{8,14},{10,12},{12,10},{14,8},{1,7},{3,5},... | collective-permute-start | bytes 786440 | tf_op jit(solution)/shard_map/ppermute | solution.py:211
  13.1 1.2 %copy-done.2 = bf16[128,4096]{1,0:T(8,128)(2,1)S(1)} copy-done((bf16[128,4096]{1,0:T(8,128)(2,1)S(1)}, bf16[128,4096]{1,0:T(8,128)(2,1)}, u32[]{:S(2)}) %copy-start.2) | copy-done | bytes 1048600
  14.6 2.1 %collective-permute-done.1.query_ref = bf16[32,4096]{1,0:T(8,128)(2,1)S(1)} collective-permute-done((bf16[32,4096]{1,0:T(8,128)(2,1)S(1)}, bf16[32,4096]{1,0:T(8,128)(2,1)S(1)}, u32[]{:S(2)}, u32[]{:S(2)}) %collective-permute-start.1) | collective-permute-done | bytes 262176 | tf_op jit(solution)/shard_map/ppermute | solution.py:211
  16.7 3.8 %collective-permute-start.6 = (bf16[32,4096]{1,0:T(8,128)(2,1)S(1)}, bf16[32,4096]{1,0:T(8,128)(2,1)S(1)}, u32[]{:S(2)}, u32[]{:S(2)}) collective-permute-start(bf16[32,4096]{1,0:T(8,128)(2,1)S(1)} %get-tuple-element.45), channel_id=1, source_target_pairs={{0,12},{2,14},{4,8},{6,10},{8,4},{10,6},{12,0},{14,2},{1,13},{3,15... | collective-permute-start | bytes 786440 | tf_op jit(solution)/shard_map/ppermute | solution.py:211
  20.5 2.1 %attend_score.8 = f32[1,1,32]{2,1,0:T(1,128)S(1)} custom-call(bf16[32,4096]{1,0:T(8,128)(2,1)S(1)} %collective-permute-done.1.query_ref, bf16[1024,512]{1,0:T(8,128)(2,1)S(1)} %copy-done, bf16[1024,512]{1,0:T(8,128)(2,1)S(1)} %copy-done.1, f32[1,4096]{1,0:T(1,128)S(1)} %bitcast.12), custom_call_target="tpu_custom_call" | custom-call | flops 1048576 | bytes 1024 | tf_op jit(solution)/shard_map/attend_score/pallas_call | solution.py:163
  22.6 2.1 %attend_score.9 = f32[1,1,32]{2,1,0:T(1,128)S(1)} custom-call(bf16[32,4096]{1,0:T(8,128)(2,1)S(1)} %get-tuple-element.37.query_ref, bf16[1024,512]{1,0:T(8,128)(2,1)S(1)} %copy-done, bf16[1024,512]{1,0:T(8,128)(2,1)S(1)} %copy-done.1, f32[1,4096]{1,0:T(1,128)S(1)} %bitcast.13), custom_call_target="tpu_custom_call" | custom-call | flops 1048576 | bytes 1024 | tf_op jit(solution)/shard_map/attend_score/pallas_call | solution.py:163
  24.7 2.3 %collective-permute-done.query_ref = bf16[32,4096]{1,0:T(8,128)(2,1)S(1)} collective-permute-done((bf16[32,4096]{1,0:T(8,128)(2,1)S(1)}, bf16[32,4096]{1,0:T(8,128)(2,1)S(1)}, u32[]{:S(2)}, u32[]{:S(2)}) %collective-permute-start) | collective-permute-done | bytes 262176 | tf_op jit(solution)/shard_map/ppermute | solution.py:211
  27.0 2.2 %attend_score.10 = f32[1,1,32]{2,1,0:T(1,128)S(1)} custom-call(bf16[32,4096]{1,0:T(8,128)(2,1)S(1)} %collective-permute-done.query_ref, bf16[1024,512]{1,0:T(8,128)(2,1)S(1)} %copy-done, bf16[1024,512]{1,0:T(8,128)(2,1)S(1)} %copy-done.1, f32[1,4096]{1,0:T(1,128)S(1)} %bitcast.14), custom_call_target="tpu_custom_call" | custom-call | flops 1048576 | bytes 1024 | tf_op jit(solution)/shard_map/attend_score/pallas_call | solution.py:163
  29.3 2.1 %attend_score.11 = f32[1,1,32]{2,1,0:T(1,128)S(1)} custom-call(bf16[32,4096]{1,0:T(8,128)(2,1)S(1)} %collective-permute-done.3.query_ref, bf16[1024,512]{1,0:T(8,128)(2,1)S(1)} %copy-done, bf16[1024,512]{1,0:T(8,128)(2,1)S(1)} %copy-done.1, f32[1,4096]{1,0:T(1,128)S(1)} %bitcast.15), custom_call_target="tpu_custom_call" | custom-call | flops 1048576 | bytes 1024 | tf_op jit(solution)/shard_map/attend_score/pallas_call | solution.py:163
  31.3 1.5 %collective-permute-done.2.query_ref = bf16[32,4096]{1,0:T(8,128)(2,1)S(1)} collective-permute-done((bf16[32,4096]{1,0:T(8,128)(2,1)S(1)}, bf16[32,4096]{1,0:T(8,128)(2,1)S(1)}, u32[]{:S(2)}, u32[]{:S(2)}) %collective-permute-start.2) | collective-permute-done | bytes 262176 | tf_op jit(solution)/shard_map/ppermute | solution.py:211
  32.8 2.1 %attend_score.12 = f32[1,1,32]{2,1,0:T(1,128)S(1)} custom-call(bf16[32,4096]{1,0:T(8,128)(2,1)S(1)} %collective-permute-done.2.query_ref, bf16[1024,512]{1,0:T(8,128)(2,1)S(1)} %copy-done, bf16[1024,512]{1,0:T(8,128)(2,1)S(1)} %copy-done.1, f32[1,4096]{1,0:T(1,128)S(1)} %bitcast.16), custom_call_target="tpu_custom_call" | custom-call | flops 1048576 | bytes 1024 | tf_op jit(solution)/shard_map/attend_score/pallas_call | solution.py:163
  34.9 2.3 %attend_score.13 = f32[1,1,32]{2,1,0:T(1,128)S(1)} custom-call(bf16[32,4096]{1,0:T(8,128)(2,1)S(1)} %collective-permute-done.4.query_ref, bf16[1024,512]{1,0:T(8,128)(2,1)S(1)} %copy-done, bf16[1024,512]{1,0:T(8,128)(2,1)S(1)} %copy-done.1, f32[1,4096]{1,0:T(1,128)S(1)} %bitcast.17), custom_call_target="tpu_custom_call" | custom-call | flops 1048576 | bytes 1024 | tf_op jit(solution)/shard_map/attend_score/pallas_call | solution.py:163
  37.3 1.4 %collective-permute-start.5 = (f32[1,128]{1,0:T(1,128)S(1)}, f32[1,128]{1,0:T(1,128)S(1)}, u32[]{:S(2)}, u32[]{:S(2)}) collective-permute-start(f32[1,128]{1,0:T(1,128)S(1)} %pad_maximum_fusion), channel_id=1, source_target_pairs={{0,2},{2,0},{4,6},{6,4},{8,10},{10,8},{12,14},{14,12},{1,3},{3,1},... | collective-permute-start | bytes 1544 | tf_op jit(solution)/shard_map/ppermute | solution.py:220
  38.7 7.7 %collective-permute-start.8 = (bf16[32,4096]{1,0:T(8,128)(2,1)S(1)}, bf16[32,4096]{1,0:T(8,128)(2,1)S(1)}, u32[]{:S(2)}, u32[]{:S(2)}) collective-permute-start(bf16[32,4096]{1,0:T(8,128)(2,1)S(1)} %get-tuple-element.47), channel_id=1, source_target_pairs={{0,8},{2,10},{4,12},{6,14},{8,0},{10,2},{12,4},{14,6},{1,9},{3,11}... | collective-permute-start | bytes 786440 | tf_op jit(solution)/shard_map/ppermute | solution.py:211
  46.4 2.1 %attend_score.14 = f32[1,1,32]{2,1,0:T(1,128)S(1)} custom-call(bf16[32,4096]{1,0:T(8,128)(2,1)S(1)} %collective-permute-done.6.query_ref, bf16[1024,512]{1,0:T(8,128)(2,1)S(1)} %copy-done, bf16[1024,512]{1,0:T(8,128)(2,1)S(1)} %copy-done.1, f32[1,4096]{1,0:T(1,128)S(1)} %bitcast.18), custom_call_target="tpu_custom_call" | custom-call | flops 1048576 | bytes 1024 | tf_op jit(solution)/shard_map/attend_score/pallas_call | solution.py:163
  48.8 5.6 %collective-permute-done.8.query_ref = bf16[32,4096]{1,0:T(8,128)(2,1)S(1)} collective-permute-done((bf16[32,4096]{1,0:T(8,128)(2,1)S(1)}, bf16[32,4096]{1,0:T(8,128)(2,1)S(1)}, u32[]{:S(2)}, u32[]{:S(2)}) %collective-permute-start.8) | collective-permute-done | bytes 262176 | tf_op jit(solution)/shard_map/ppermute | solution.py:211
  54.4 2.1 %attend_score.15 = f32[1,1,32]{2,1,0:T(1,128)S(1)} custom-call(bf16[32,4096]{1,0:T(8,128)(2,1)S(1)} %collective-permute-done.8.query_ref, bf16[1024,512]{1,0:T(8,128)(2,1)S(1)} %copy-done, bf16[1024,512]{1,0:T(8,128)(2,1)S(1)} %copy-done.1, f32[1,4096]{1,0:T(1,128)S(1)} %bitcast.19), custom_call_target="tpu_custom_call" | custom-call | flops 1048576 | bytes 1024 | tf_op jit(solution)/shard_map/attend_score/pallas_call | solution.py:163
  56.6 2.3 %collective-permute-start.9 = (f32[1,128]{1,0:T(1,128)S(1)}, f32[1,128]{1,0:T(1,128)S(1)}, u32[]{:S(2)}, u32[]{:S(2)}) collective-permute-start(f32[1,128]{1,0:T(1,128)S(1)} %pad_maximum_fusion.2), channel_id=1, source_target_pairs={{0,8},{2,10},{4,12},{6,14},{8,0},{10,2},{12,4},{14,6},{1,9},{3,11}... | collective-permute-start | bytes 1544 | tf_op jit(solution)/shard_map/ppermute | solution.py:220
  59.0 2.1 %collective-permute-done.9 = f32[1,128]{1,0:T(1,128)S(1)} collective-permute-done((f32[1,128]{1,0:T(1,128)S(1)}, f32[1,128]{1,0:T(1,128)S(1)}, u32[]{:S(2)}, u32[]{:S(2)}) %collective-permute-start.9) | collective-permute-done | bytes 544 | tf_op jit(solution)/shard_map/ppermute | solution.py:220
  61.6 1.1 %collective-permute-done.10 = f32[128]{0:T(128)S(1)} collective-permute-done((f32[128]{0:T(128)S(1)}, f32[128]{0:T(128)S(1)}, u32[]{:S(2)}, u32[]{:S(2)}) %collective-permute-start.10) | collective-permute-done | bytes 544 | tf_op jit(solution)/shard_map/ppermute | solution.py:249
  (30 shorter events, 1.9 us)
Async XLA Ops:
  0.0 0.7 %copy-start.5 = (s32[128,1]{0,1:T(1,128)S(1)}, s32[128,1]{0,1:T(1,128)}, u32[]{:S(2)}) copy-start(s32[128,1]{0,1:T(1,128)} %param.7) | copy-start | bytes 1540
  0.0 0.7 %copy-start.4 = (s32[8]{0:T(128)S(1)}, s32[8]{0:T(128)}, u32[]{:S(2)}) copy-start(s32[8]{0:T(128)} %owner_hbm.1) | copy-start | bytes 100
  0.7 19.9 %copy-start = (bf16[1024,512]{1,0:T(8,128)(2,1)S(1)}, bf16[1024,512]{1,0:T(8,128)(2,1)}, u32[]{:S(2)}) copy-start(bf16[1024,512]{1,0:T(8,128)(2,1)} %key_ref.7) | copy-start | bytes 3145732
  0.7 19.9 %copy-start.1 = (bf16[1024,512]{1,0:T(8,128)(2,1)S(1)}, bf16[1024,512]{1,0:T(8,128)(2,1)}, u32[]{:S(2)}) copy-start(bf16[1024,512]{1,0:T(8,128)(2,1)} %value_ref.7) | copy-start | bytes 3145732
  3.5 13.2 %collective-permute-start.1 = (bf16[32,4096]{1,0:T(8,128)(2,1)S(1)}, bf16[32,4096]{1,0:T(8,128)(2,1)S(1)}, u32[]{:S(2)}, u32[]{:S(2)}) collective-permute-start(bf16[32,4096]{1,0:T(8,128)(2,1)S(1)} %get-tuple-element.33), channel_id=1, source_target_pairs={{0,14},{2,12},{4,10},{6,8},{8,6},{10,4},{12,2},{14,0},{1,15},{3,13... | collective-permute-start | bytes 786440 | tf_op jit(solution)/shard_map/ppermute | solution.py:211
  9.6 17.5 %collective-permute-start = (bf16[32,4096]{1,0:T(8,128)(2,1)S(1)}, bf16[32,4096]{1,0:T(8,128)(2,1)S(1)}, u32[]{:S(2)}, u32[]{:S(2)}) collective-permute-start(bf16[32,4096]{1,0:T(8,128)(2,1)S(1)} %get-tuple-element.30), channel_id=1, source_target_pairs={{0,2},{2,0},{4,6},{6,4},{8,10},{10,8},{12,14},{14,12},{1,3},{3,1},... | collective-permute-start | bytes 786440 | tf_op jit(solution)/shard_map/ppermute | solution.py:211
  10.1 19.2 %collective-permute-start.3 = (bf16[32,4096]{1,0:T(8,128)(2,1)S(1)}, bf16[32,4096]{1,0:T(8,128)(2,1)S(1)}, u32[]{:S(2)}, u32[]{:S(2)}) collective-permute-start(bf16[32,4096]{1,0:T(8,128)(2,1)S(1)} %get-tuple-element.40), channel_id=1, source_target_pairs={{0,4},{2,6},{4,0},{6,2},{8,12},{10,14},{12,8},{14,10},{1,5},{3,7},... | collective-permute-start | bytes 786440 | tf_op jit(solution)/shard_map/ppermute | solution.py:211
  10.1 22.7 %collective-permute-start.2 = (bf16[32,4096]{1,0:T(8,128)(2,1)S(1)}, bf16[32,4096]{1,0:T(8,128)(2,1)S(1)}, u32[]{:S(2)}, u32[]{:S(2)}) collective-permute-start(bf16[32,4096]{1,0:T(8,128)(2,1)S(1)} %get-tuple-element.39), channel_id=1, source_target_pairs={{0,6},{2,4},{4,2},{6,0},{8,14},{10,12},{12,10},{14,8},{1,7},{3,5},... | collective-permute-start | bytes 786440 | tf_op jit(solution)/shard_map/ppermute | solution.py:211
  13.1 21.8 %collective-permute-start.4 = (bf16[32,4096]{1,0:T(8,128)(2,1)S(1)}, bf16[32,4096]{1,0:T(8,128)(2,1)S(1)}, u32[]{:S(2)}, u32[]{:S(2)}) collective-permute-start(bf16[32,4096]{1,0:T(8,128)(2,1)S(1)} %get-tuple-element.43), channel_id=1, source_target_pairs={{0,10},{2,8},{4,14},{6,12},{8,2},{10,0},{12,6},{14,4},{1,11},{3,9}... | collective-permute-start | bytes 786440 | tf_op jit(solution)/shard_map/ppermute | solution.py:211
  13.1 1.2 %copy-start.2 = (bf16[128,4096]{1,0:T(8,128)(2,1)S(1)}, bf16[128,4096]{1,0:T(8,128)(2,1)}, u32[]{:S(2)}) copy-start(bf16[128,4096]{1,0:T(8,128)(2,1)} %get-tuple-element.31.query_ref) | copy-start | bytes 3145732
  14.3 6.3 %copy-start.3 = (f32[4096]{0:T(1024)S(1)}, f32[4096]{0:T(1024)}, u32[]{:S(2)}) copy-start(f32[4096]{0:T(1024)} %param.11) | copy-start | bytes 49156
  16.7 29.6 %collective-permute-start.6 = (bf16[32,4096]{1,0:T(8,128)(2,1)S(1)}, bf16[32,4096]{1,0:T(8,128)(2,1)S(1)}, u32[]{:S(2)}, u32[]{:S(2)}) collective-permute-start(bf16[32,4096]{1,0:T(8,128)(2,1)S(1)} %get-tuple-element.45), channel_id=1, source_target_pairs={{0,12},{2,14},{4,8},{6,10},{8,4},{10,6},{12,0},{14,2},{1,13},{3,15... | collective-permute-start | bytes 786440 | tf_op jit(solution)/shard_map/ppermute | solution.py:211
  37.3 11.2 %collective-permute-start.5 = (f32[1,128]{1,0:T(1,128)S(1)}, f32[1,128]{1,0:T(1,128)S(1)}, u32[]{:S(2)}, u32[]{:S(2)}) collective-permute-start(f32[1,128]{1,0:T(1,128)S(1)} %pad_maximum_fusion), channel_id=1, source_target_pairs={{0,2},{2,0},{4,6},{6,4},{8,10},{10,8},{12,14},{14,12},{1,3},{3,1},... | collective-permute-start | bytes 1544 | tf_op jit(solution)/shard_map/ppermute | solution.py:220
  38.7 15.7 %collective-permute-start.8 = (bf16[32,4096]{1,0:T(8,128)(2,1)S(1)}, bf16[32,4096]{1,0:T(8,128)(2,1)S(1)}, u32[]{:S(2)}, u32[]{:S(2)}) collective-permute-start(bf16[32,4096]{1,0:T(8,128)(2,1)S(1)} %get-tuple-element.47), channel_id=1, source_target_pairs={{0,8},{2,10},{4,12},{6,14},{8,0},{10,2},{12,4},{14,6},{1,9},{3,11}... | collective-permute-start | bytes 786440 | tf_op jit(solution)/shard_map/ppermute | solution.py:211
  48.6 7.9 %collective-permute-start.7 = (f32[1,128]{1,0:T(1,128)S(1)}, f32[1,128]{1,0:T(1,128)S(1)}, u32[]{:S(2)}, u32[]{:S(2)}) collective-permute-start(f32[1,128]{1,0:T(1,128)S(1)} %pad_maximum_fusion.1), channel_id=1, source_target_pairs={{0,4},{2,6},{4,0},{6,2},{8,12},{10,14},{12,8},{14,10},{1,5},{3,7},... | collective-permute-start | bytes 1544 | tf_op jit(solution)/shard_map/ppermute | solution.py:220
  56.6 4.4 %collective-permute-start.9 = (f32[1,128]{1,0:T(1,128)S(1)}, f32[1,128]{1,0:T(1,128)S(1)}, u32[]{:S(2)}, u32[]{:S(2)}) collective-permute-start(f32[1,128]{1,0:T(1,128)S(1)} %pad_maximum_fusion.2), channel_id=1, source_target_pairs={{0,8},{2,10},{4,12},{6,14},{8,0},{10,2},{12,4},{14,6},{1,9},{3,11}... | collective-permute-start | bytes 1544 | tf_op jit(solution)/shard_map/ppermute | solution.py:220
  61.5 1.2 %collective-permute-start.10 = (f32[128]{0:T(128)S(1)}, f32[128]{0:T(128)S(1)}, u32[]{:S(2)}, u32[]{:S(2)}) collective-permute-start(f32[128]{0:T(128)S(1)} %select_reduce_fusion), channel_id=1, source_target_pairs={{0,1},{1,0},{2,3},{3,2},{4,5},{5,4},{6,7},{7,6},{8,9},{9,8},{10,11... | collective-permute-start | bytes 1544 | tf_op jit(solution)/shard_map/ppermute | solution.py:249
